TPU v7x, 1024 devices: a whole 4x8x16 slice. The times are simulated.
1024 devices in a mesh: aux: 16 (over x, y_lo, core), blk: 64 (over y_hi, z).
Axes of the slice: x: 4, y: 8 (y_hi: 4, y_lo: 2; y = y_hi * 2 + y_lo), z: 16, core: 2. Of those that a mesh axis runs over, the one named last changes fastest.
Arguments:
- b_tensor: bfloat16 [64, 16, 256, 128], P('blk', None, 'aux'), may hold values from -2 to 2
- significance: int32 [64, 16, 2], P(None, 'aux'), may hold values from 0 to 1, as said below
- pair_keep: int32 [16, 64, 64], P('aux'), may hold values 0 or 1
- occ_energy: float32 [64, 16], P(None, 'aux'), may hold values from -1.2 to -0.3
- virt_energy: float32 [16, 128], P('aux'), may hold values from 0.3 to 2.5
Outputs:
- gamma: float32 [64, 16, 256, 128], P('blk', None, 'aux')
Inputs may be any that keep to these rules, and one draw needn't show every extreme that they name: `significance`: every orbital has at least one significant block among its 2.
All inputs are finite; a program needn't handle non-finite values. No bound on the sum of `pair_keep` on one device may be relied on, other than what follows from the above.
Results may differ from a plain program's by a relative error of at most 0.00062.
Values may be sent and summed in bfloat16 or wider, within the bound.
No kernel may reach another device: no remote copies, remote signals or barrier semaphores. Data moves between devices by JAX's collectives and lax.ppermute only.
A program may use at most 32 MiB of HBM per device.

v0:
```python
import jax
import jax.numpy as jnp
from jax import lax
from jax.sharding import PartitionSpec as P

ABLK = 128


def pair_terms(own, others, e_own, e_others, keep_others, virtual):
    ints = jnp.einsum("xa,kxb->kab", own, others, preferred_element_type=jnp.float32)
    denom = e_own + e_others[:, None, None] - virtual[None, :, None] - virtual[None, None, :]
    amp = keep_others[:, None, None] * ints / denom
    return (2.0 * amp - jnp.swapaxes(amp, 1, 2)).astype(jnp.bfloat16)


def on_device(b_tensor, significance, pair_keep, occ_energy, virt_energy):
    mine = lax.all_to_all(b_tensor, "aux", split_axis=1, concat_axis=2, tiled=True)
    position = lax.axis_index("blk")
    count = lax.axis_size("blk")
    mask_all = jnp.repeat(significance[:, 0, :], ABLK, axis=1)
    own_mask = lax.dynamic_index_in_dim(mask_all, position, 0, keepdims=False)
    own = jnp.where(own_mask[:, None] > 0, mine[0, 0], jnp.zeros((), mine.dtype))
    keep = pair_keep[0]
    rows = jnp.arange(count, dtype=jnp.int32)
    upper = rows[None, :] >= rows[:, None]
    keep_row = lax.dynamic_index_in_dim(
        jnp.where(upper, keep, keep.T), position, 0, keepdims=False
    ).astype(jnp.float32)
    occupied = occ_energy[:, 0]
    e_own = lax.dynamic_index_in_dim(occupied, position, 0, keepdims=False)
    virtual = virt_energy[0]
    piece = lax.all_gather(own[None], "blk", axis=0, tiled=True)
    tilde = pair_terms(own, piece, e_own, occupied, keep_row, virtual)
    gamma = jnp.einsum("kab,kxb->xa", tilde, piece, preferred_element_type=jnp.float32)
    gamma = gamma * own_mask[:, None].astype(jnp.float32)
    return lax.all_to_all(gamma[None, None], "aux", split_axis=2, concat_axis=1, tiled=True)


def solution(mesh):
    return jax.shard_map(
        on_device,
        mesh=mesh,
        in_specs=(
            P("blk", None, "aux", None),
            P(None, "aux", None),
            P("aux", None, None),
            P(None, "aux"),
            P("aux", None),
        ),
        out_specs=P("blk", None, "aux", None),
        check_vma=False,
    )
```

profile of v0, /device:TPU:1, one launch (start us, length us, event | category | flops | bytes accessed | tf_op | source)
XLA Modules:
  0.0 221.8 jit_solution(15777481727590228328)
XLA Ops:
  6.5 17.4 %all-to-all-start = ((bf16[1,16,16,128]{3,2,0,1:T(8,128)(2,1)}), bf16[1,16,16,128]{3,2,0,1:T(8,128)(2,1)S(1)}, u32[]{:S(2)}, u32[]{:S(2)}) async-start(bf16[1,16,16,128]{3,2,0,1:T(8,128)(2,1)} %bitcast.50), calls=%async_computation | async-start | bytes 131072 | tf_op jit(solution)/shard_map/all_to_all | solution.py:17
  24.0 0.0 all-gather.2.cloned.1.call-start
  24.0 0.8 copy.16
  24.8 0.1 broadcast_in_dim.28
  25.0 4.9 %all-to-all-done = bf16[1,16,16,128]{3,2,0,1:T(8,128)(2,1)S(1)} async-done(((bf16[1,16,16,128]{3,2,0,1:T(8,128)(2,1)}), bf16[1,16,16,128]{3,2,0,1:T(8,128)(2,1)S(1)}, u32[]{:S(2)}, u32[]{:S(2)}) %all-to-all-start) | async-done | bytes 65568 | tf_op jit(solution)/shard_map/all_to_all | solution.py:17
  29.9 0.7 broadcast_select_fusion
  30.6 0.0 all-gather.2.cloned.1.call-update
  30.6 1.2 constant_dynamic-slice_fusion.1
  31.9 0.8 copy.18
  32.7 0.7 convert_bitcast_fusion
  33.4 1.2 add_bitcast_fusion
  34.6 0.7 broadcast_subtract_fusion
  35.3 0.1 bitcast_select_fusion
  35.5 142.5 %all-gather.2.cloned.1.call-done = bf16[64,256,128]{2,1,0:T(8,128)(2,1)} async-done(((bf16[1,256,128]{2,1,0:T(8,128)(2,1)}), bf16[64,256,128]{2,1,0:T(8,128)(2,1)}) %all-gather.2.cloned.1.call-update) | async-done | bytes 4194320 | tf_op jit(solution)/shard_map/all_gather | solution.py:32
  178.0 5.6 %convolution_multiply_fusion = f32[64,128,128]{2,1,0:T(8,128)} fusion(bf16[64,256,128]{2,1,0:T(8,128)(2,1)} %all-gather.2.cloned.1.call-done, f32[64]{0:T(128)S(1)} %convert_bitcast_fusion, bf16[256,128]{1,0:T(8,128)(2,1)S(1)} %bitcast_select_fusion), kind=kOutput, calls=%fused_computation.4 | convolution fusion | flops 537919488 | bytes 8454400 | tf_op jit(solution)/shard_map/xa,kxb->kab/dot_general | solution.py:10
  183.6 0.0 copy-start
  183.6 5.6 %copy.20 = f32[64,128,128]{1,2,0:T(8,128)} copy(f32[64,128,128]{2,1,0:T(8,128)} %convolution_multiply_fusion) | data formatting | bytes 8388608 | tf_op jit(solution)/shard_map/mul | solution.py:12
  189.2 0.0 copy-done
  189.2 5.6 %fusion.8 = f32[256,128]{1,0:T(8,128)S(1)} fusion(bf16[64,256,128]{2,1,0:T(8,128)(2,1)} %all-gather.2.cloned.1.call-done, f32[64,128,128]{1,2,0:T(8,128)} %copy.20, f32[64,128,128]{2,1,0:T(8,128)} %convolution_multiply_fusion, f32[128]{0:T(128)S(1)} %bitcast.57, f32[64,128]{1,0:T(8,128)S(1)} %broadcast_subtract_fusion, f32[256]{0:T(256)S(1)} %bitcast.55), kind=kOutput, calls=%fused_computation.7 | convolution fusion | flops 544243712 | bytes 12748288 | tf_op jit(solution)/shard_map/kab,kxb->xa/dot_general | solution.py:34
  194.9 19.4 %all_to_all.21 = f32[1,1,256,128]{3,1,0,2:T(1,128)S(1)} all-to-all(f32[1,1,256,128]{3,1,0,2:T(1,128)S(1)} %bitcast.47), channel_id=1, replica_groups=mesh['aux'=16,'blk'=64] {'aux'}, dimensions={2} | all-to-all | bytes 262144 | tf_op jit(solution)/shard_map/all_to_all | solution.py:36
  214.3 0.7 copy.27
  (3 shorter events, 0.0 us)
Async XLA Ops:
  6.5 23.3 %all-to-all-start = ((bf16[1,16,16,128]{3,2,0,1:T(8,128)(2,1)}), bf16[1,16,16,128]{3,2,0,1:T(8,128)(2,1)S(1)}, u32[]{:S(2)}, u32[]{:S(2)}) async-start(bf16[1,16,16,128]{3,2,0,1:T(8,128)(2,1)} %bitcast.50), calls=%async_computation | async-start | bytes 131072 | tf_op jit(solution)/shard_map/all_to_all | solution.py:17
  24.0 154.0 %all-gather.2.cloned.1.call-start = ((), (), s32[]{:S(2)}) async-start(), calls=%async_computation.2 | async-start | bytes 4259840 | tf_op jit(solution)/shard_map/all_gather | solution.py:32
  183.6 5.6 %copy-start = (f32[1,128]{1,0:T(1,128)S(1)}, f32[1,128]{1,0:T(1,128)}, u32[]{:S(2)}) copy-start(f32[1,128]{1,0:T(1,128)} %param.9) | copy-start | bytes 1540
Sparse Core Ops, SparseCore 0:
  30.7 147.1 all-gather.1
where the time goes:
time: 222 us
  waiting for transfers between devices  147 us (66%)
  blocking collectives  19.4 us (9%)
  starting transfers between devices  17.5 us (8%)
  between operations  13.4 us (6%)
  matrix products  11.3 us (5%)
  local copies, waits for them, and re-layouts  9.23 us (4%)
  other arithmetic  3.52 us (2%)
    all_gather x1, waiting for transfers between devices, on_device(): piece = lax.all_gather(own[None], 'blk', axis=0, tiled=True)  143 us
    all_to_all x1, blocking collectives, on_device(): lax.all_to_all(gamma[None, None], 'aux', split_axis=2, concat_axis=1, til...  19.4 us
    all_to_all x1, starting transfers between devices, on_device(): lax.all_to_all(b_tensor, 'aux', split_axis=1, concat_axis=2, tiled=True)  17.4 us
    dot_general x1, matrix products, on_device(): jnp.einsum('kab,kxb->xa', tilde, piece, preferred_element_type=jnp.float32)  5.65 us
    dot_general x1, matrix products, pair_terms(): jnp.einsum('xa,kxb->kab', own, others, preferred_element_type=jnp.float32)  5.63 us
    mul x1, local copies, waits for them, and re-layouts, pair_terms(): amp = keep_others[:, None, None] * ints / denom  5.61 us
    all_to_all x1, waiting for transfers between devices, on_device(): lax.all_to_all(b_tensor, 'aux', split_axis=1, concat_axis=2, tiled=True)  4.89 us
  transfers between devices with their start and end apart: 2, of which 2 were waited for; matrix products, arithmetic and copies ran while one was open for 3% of the time, Pallas kernels for 0%

commit v1 on v0

v1 whole, which is shorter than its diff:
```python
import jax
import jax.numpy as jnp
from jax import lax
from jax.experimental import pallas as pl
from jax.experimental.pallas import tpu as pltpu
from jax.sharding import Mesh, PartitionSpec as P

AUX = ("aux_x", "aux_y", "aux_core")
NP = 4
NH = 4
NL = 4
NZ = NH * NL
NC = NZ // 2
V = 128
AB = 128
NA = 256


def pair_kernel(sig, keep, occ, virt, p_ref, q0, q1, q2a, q2b, q3, out, pcat, pcat_t, qcat, vb, acc):
    h = lax.axis_index("blk_y")
    near = lax.axis_index("blk_near")
    rows = lax.broadcasted_iota(jnp.int32, (NA, V), 0)
    zero = jnp.zeros((NA, V), jnp.bfloat16)

    def masked(block, orbital):
        live = jnp.where(rows < AB, sig[0, orbital], sig[1, orbital]) > 0
        return jnp.where(live, block, zero)

    def q_index(chunk, t):
        far = 2 * lax.rem(chunk, 2) + t
        return h * NZ + far * NL + lax.rem(near + lax.div(chunk, 2), NL)

    w = lax.axis_index("blk_far") * NL + near
    p_index = [s * NZ + w for s in range(NP)]
    for s in range(NP):
        block = masked(p_ref[s], p_index[s])
        pcat[:, s * V : (s + 1) * V] = block
        pcat_t[s * V : (s + 1) * V, :] = block.T
    halves = [(q0, 0), (q0, 2), (q1, 0), (q1, 2), (q2a, 0), (q2b, 0), (q3, 0), (q3, 2)]
    for c, (ref, first) in enumerate(halves):
        for t in range(2):
            qcat[c, :, t * V : (t + 1) * V] = masked(ref[first + t], q_index(c, t))
    va = virt[...]
    vb[...] = jnp.broadcast_to(va, (V, V)).T
    acc[...] = jnp.zeros_like(acc)

    @pl.loop(0, NC)
    def chunk(c):
        block = qcat[c]
        x = jnp.dot(block.T, pcat[...], preferred_element_type=jnp.float32)
        y = jnp.dot(pcat_t[...], block, preferred_element_type=jnp.float32)
        columns = []
        for s in range(NP):
            tiles = []
            for t in range(2):
                p, q = p_index[s], q_index(c, t)
                kept = keep[lax.min(p, q), lax.max(p, q)].astype(jnp.float32)
                total = occ[0, p] + occ[0, q]
                xt = x[t * V : (t + 1) * V, s * V : (s + 1) * V]
                yt = y[s * V : (s + 1) * V, t * V : (t + 1) * V]
                denom = (total - va) - vb[...]
                tiles.append((kept * (2.0 * xt - yt) / denom).astype(jnp.bfloat16))
            columns.append(jnp.concatenate(tiles, axis=0))
        tilde = jnp.concatenate(columns, axis=1)
        acc[...] += jnp.dot(block, tilde, preferred_element_type=jnp.float32)

    for s in range(NP):
        live = jnp.where(rows < AB, sig[0, p_index[s]], sig[1, p_index[s]]) > 0
        gamma = jnp.where(live, acc[:, s * V : (s + 1) * V], 0.0)
        out[:, s] = gamma.reshape(16, 16, V)


def pairs(sig, keep, occ, virt, *blocks):
    smem = pl.BlockSpec(memory_space=pltpu.SMEM)
    vmem = pl.BlockSpec(memory_space=pltpu.VMEM)
    return pl.pallas_call(
        pair_kernel,
        out_shape=jax.ShapeDtypeStruct((16, NP, 16, V), jnp.float32),
        in_specs=[smem] * 3 + [vmem] * (1 + len(blocks)),
        out_specs=vmem,
        scratch_shapes=[
            pltpu.VMEM((NA, NP * V), jnp.bfloat16),
            pltpu.VMEM((NP * V, NA), jnp.bfloat16),
            pltpu.VMEM((NC, NA, 2 * V), jnp.bfloat16),
            pltpu.VMEM((V, V), jnp.float32),
            pltpu.VMEM((NA, NP * V), jnp.float32),
        ],
        compiler_params=pltpu.CompilerParams(vmem_limit_bytes=24 * 2**20),
        cost_estimate=pl.CostEstimate(flops=2 * 10**9, bytes_accessed=2 * 10**6, transcendentals=10**6),
    )(sig, keep, occ, virt, *blocks)


def spread(x, axis, size):
    return lax.all_to_all(jnp.broadcast_to(x, (size,) + x.shape), axis, 0, 0, tiled=True)


def ahead(x, shift):
    pairs = [(i, (i - shift) % NZ) for i in range(NZ)]
    return lax.ppermute(x, ("blk_far", "blk_near"), pairs)


def on_device(b_tensor, significance, pair_keep, occ_energy, virt_energy):
    own = lax.all_to_all(b_tensor[0], AUX, 0, 0, tiled=True).reshape(NA, V)
    q0 = spread(own, "blk_far", NH)
    p_blocks = spread(own, "blk_y", NP)
    q1, q3 = ahead(q0, 1), ahead(q0, -1)
    q2a, q2b = ahead(q0[:2], 2), ahead(q0[2:], -2)
    part = pairs(
        significance[:, 0, :].T, pair_keep[0], occ_energy.T, virt_energy, p_blocks, q0, q1, q2a, q2b, q3
    )
    back = lax.all_to_all(part.reshape(64, 16, V), AUX + ("blk_y",), 0, 0, tiled=True)
    return back.reshape(16, NP, 16, V).sum(axis=1)[None]


def solution(mesh):
    blk = ("blk_y", "blk_far", "blk_near")
    fine = Mesh(mesh.devices.reshape(4, 2, 2, NP, NH, NL), AUX + blk)
    return jax.shard_map(
        on_device,
        mesh=fine,
        in_specs=(
            P(blk, None, AUX, None),
            P(None, AUX, None),
            P(AUX, None, None),
            P(None, AUX),
            P(AUX, None),
        ),
        out_specs=P(blk, None, AUX, None),
        check_vma=False,
    )
```

time: 222 us -> 115 us (0.52)
  waiting for transfers between devices: 147 us -> 8.34 us
  blocking collectives: 19.4 us -> 73.1 us
  between operations: 13.4 us -> 0.1 us
  matrix products: 11.3 us -> 0 us
  local copies, waits for them, and re-layouts: 9.23 us -> 1.41 us
  starting transfers between devices: 17.5 us -> 24.9 us
  Pallas kernels: 0 us -> 6.34 us
  other arithmetic: 3.52 us -> 0.69 us
    all_gather x1 -> x0, waiting for transfers between devices: 143 us -> none  [on_device(): piece = lax.all_gather(own[None], 'blk', axis=0, tiled=True)]
    all_to_all x1 -> x3, blocking collectives: 19.4 us -> 73.1 us  [the longest x1 27.6 us: on_device(): lax.all_to_all(part.reshape(64, 16, V), AUX + ('blk_y',), 0, 0, tiled=True)]
    ppermute x0 -> x4, starting transfers between devices: none -> 19 us  [ahead(): return lax.ppermute(x, ('blk_far', 'blk_near'), pairs)]
    all_to_all x1, starting transfers between devices: 17.4 us -> 5.92 us  [spread(): lax.all_to_all(jnp.broadcast_to(x, (size,) + x.shape), axis, 0, 0, tiled=...]
    dot_general x2 -> x0, matrix products: 11.3 us -> none  [the longest x1 5.65 us: on_device(): jnp.einsum('kab,kxb->xa', tilde, piece, preferred_element_type=jnp.float32)]
    ppermute x0 -> x4, waiting for transfers between devices: none -> 8.34 us  [ahead(): return lax.ppermute(x, ('blk_far', 'blk_near'), pairs)]
    pallas_call x0 -> x1, Pallas kernels: none -> 6.34 us  [pairs(): pl.pallas_call(pair_kernel, out_shape=jax.ShapeDtypeStruct((16, NP, 16, V...]
    mul x1 -> x0, local copies, waits for them, and re-layouts: 5.61 us -> none  [pair_terms(): amp = keep_others[:, None, None] * ints / denom]
  transfers between devices with their start and end apart: 2 -> 5, of which waited for: 2 -> 2; matrix products, arithmetic and copies ran while one was open for 3% -> 0% of each run, Pallas kernels for 0% -> 0%
where the time goes in v1:
time: 115 us
  blocking collectives  73.1 us (64%)
  starting transfers between devices  24.9 us (22%)
  waiting for transfers between devices  8.34 us (7%)
  Pallas kernels  6.34 us (6%)
  local copies, waits for them, and re-layouts  1.41 us (1%)
    all_to_all x1, blocking collectives, on_device(): lax.all_to_all(part.reshape(64, 16, V), AUX + ('blk_y',), 0, 0, tiled=True)  27.6 us
    all_to_all x1, blocking collectives, on_device(): own = lax.all_to_all(b_tensor[0], AUX, 0, 0, tiled=True).reshape(NA, V)  23.3 us
    all_to_all x1, blocking collectives, spread(): lax.all_to_all(jnp.broadcast_to(x, (size,) + x.shape), axis, 0, 0, tiled=...  22.1 us
    ppermute x4, starting transfers between devices, ahead(): return lax.ppermute(x, ('blk_far', 'blk_near'), pairs)  19 us
    ppermute x4, waiting for transfers between devices, ahead(): return lax.ppermute(x, ('blk_far', 'blk_near'), pairs)  8.34 us
    pallas_call x1, Pallas kernels, pairs(): pl.pallas_call(pair_kernel, out_shape=jax.ShapeDtypeStruct((16, NP, 16, V...  6.34 us
    all_to_all x1, starting transfers between devices, spread(): lax.all_to_all(jnp.broadcast_to(x, (size,) + x.shape), axis, 0, 0, tiled=...  5.92 us
  transfers between devices with their start and end apart: 5, of which 2 were waited for; matrix products, arithmetic and copies ran while one was open for 0% of the time, Pallas kernels for 0%

profile of v1, /device:TPU:1, one launch (start us, length us, event | category | flops | bytes accessed | tf_op | source)
XLA Modules:
  0.0 114.9 jit_solution(118127951831743794)
XLA Ops:
  0.0 23.3 %all_to_all.20 = bf16[16,16,128]{2,1,0:T(8,128)(2,1)S(1)} all-to-all(bf16[16,16,128]{2,1,0:T(8,128)(2,1)} %bitcast.16), channel_id=1, replica_groups=mesh['aux_x'=4,'aux_y'=2,'aux_core'=2,'blk_y'=4,'blk_far'=4,'blk_near'=4..., dimensions={0} | all-to-all | bytes 131072 | tf_op jit(solution)/shard_map/all_to_all | solution.py:103
  23.3 0.7 broadcast_in_dim.7
  24.0 22.1 %all_to_all.21.q0 = bf16[4,256,128]{2,1,0:T(8,128)(2,1)S(1)} all-to-all(bf16[4,256,128]{2,1,0:T(8,128)(2,1)} %broadcast_in_dim.7), channel_id=1, replica_groups=mesh['aux_x'=4,'aux_y'=2,'aux_core'=2,'blk_y'=4,'blk_far'=4,'blk_near'=4..., dimensions={0} | all-to-all | bytes 524288 | tf_op jit(solution)/shard_map/all_to_all | solution.py:94
  46.2 5.9 %all-to-all-start.1 = ((bf16[4,256,128]{2,1,0:T(8,128)(2,1)}), bf16[4,256,128]{2,1,0:T(8,128)(2,1)S(1)}, u32[]{:S(2)}, u32[]{:S(2)}) async-start(bf16[4,256,128]{2,1,0:T(8,128)(2,1)} %broadcast_in_dim.7), calls=%async_computation.1 | async-start | bytes 524288 | tf_op jit(solution)/shard_map/all_to_all | solution.py:94
  52.1 0.0 copy-start
  52.1 8.1 %collective-permute-start.3 = (bf16[4,256,128]{2,1,0:T(8,128)(2,1)S(1)}, bf16[4,256,128]{2,1,0:T(8,128)(2,1)S(1)}, u32[]{:S(2)}, u32[]{:S(2)}) collective-permute-start(bf16[4,256,128]{2,1,0:T(8,128)(2,1)S(1)} %all_to_all.21.q0), channel_id=1, source_target_pairs={{0,1},{1,2},{2,3},{3,4},{4,5},{5,6},{6,7},{7,8},{8,9},{9,10},{10,1... | collective-permute-start | bytes 786440 | tf_op jit(solution)/shard_map/ppermute | solution.py:99
  60.2 2.9 %collective-permute-start = (bf16[4,256,128]{2,1,0:T(8,128)(2,1)S(1)}, bf16[4,256,128]{2,1,0:T(8,128)(2,1)S(1)}, u32[]{:S(2)}, u32[]{:S(2)}) collective-permute-start(bf16[4,256,128]{2,1,0:T(8,128)(2,1)S(1)} %all_to_all.21.q0), channel_id=1, source_target_pairs={{0,15},{1,0},{2,1},{3,2},{4,3},{5,4},{6,5},{7,6},{8,7},{9,8},{10,9... | collective-permute-start | bytes 786440 | tf_op jit(solution)/shard_map/ppermute | solution.py:99
  63.1 0.0 copy-start.3
  63.1 6.1 %collective-permute-start.2 = (bf16[2,256,128]{2,1,0:T(8,128)(2,1)S(1)}, bf16[2,256,128]{2,1,0:T(8,128)(2,1)S(1)}, u32[]{:S(2)}, u32[]{:S(2)}) collective-permute-start(bf16[2,256,128]{2,1,0:T(8,128)(2,1)S(1)} %get-tuple-element.5), channel_id=1, source_target_pairs={{0,2},{1,3},{2,4},{3,5},{4,6},{5,7},{6,8},{7,9},{8,10},{9,11},{10,... | collective-permute-start | bytes 393224 | tf_op jit(solution)/shard_map/ppermute | solution.py:99
  69.3 1.9 %collective-permute-start.1 = (bf16[2,256,128]{2,1,0:T(8,128)(2,1)S(1)}, bf16[2,256,128]{2,1,0:T(8,128)(2,1)S(1)}, u32[]{:S(2)}, u32[]{:S(2)}) collective-permute-start(bf16[2,256,128]{2,1,0:T(8,128)(2,1)S(1)} %get-tuple-element.6), channel_id=1, source_target_pairs={{0,14},{1,15},{2,0},{3,1},{4,2},{5,3},{6,4},{7,5},{8,6},{9,7},{10,... | collective-permute-start | bytes 393224 | tf_op jit(solution)/shard_map/ppermute | solution.py:99
  71.2 0.0 all-to-all-done.1.p_ref
  71.2 1.2 %collective-permute-done.2.q2b = bf16[2,256,128]{2,1,0:T(8,128)(2,1)S(1)} collective-permute-done((bf16[2,256,128]{2,1,0:T(8,128)(2,1)S(1)}, bf16[2,256,128]{2,1,0:T(8,128)(2,1)S(1)}, u32[]{:S(2)}, u32[]{:S(2)}) %collective-permute-start.2) | collective-permute-done | bytes 131104 | tf_op jit(solution)/shard_map/ppermute | solution.py:99
  72.3 7.2 %collective-permute-done.1.q2a = bf16[2,256,128]{2,1,0:T(8,128)(2,1)S(1)} collective-permute-done((bf16[2,256,128]{2,1,0:T(8,128)(2,1)S(1)}, bf16[2,256,128]{2,1,0:T(8,128)(2,1)S(1)}, u32[]{:S(2)}, u32[]{:S(2)}) %collective-permute-start.1) | collective-permute-done | bytes 131104 | tf_op jit(solution)/shard_map/ppermute | solution.py:99
  79.5 0.0 collective-permute-done.3.q3
  79.5 0.0 collective-permute-done.q1
  79.5 0.0 copy-start.1
  79.5 0.0 copy-start.2
  79.5 0.0 copy-done
  79.6 0.0 copy-done.3
  79.6 0.6 copy-done.1
  80.2 0.0 copy-done.2
  80.2 6.3 %shard_map.55 = f32[16,4,16,128]{3,2,1,0:T(8,128)S(1)} custom-call(s32[2,64]{1,0:T(2,128)S(1)} %bitcast.13, s32[64,64]{1,0:T(8,128)S(1)} %bitcast.12, f32[1,64]{1,0:T(1,128)S(1)} %bitcast.14, f32[1,128]{1,0:T(1,128)S(1)} %copy-done.3, bf16[4,256,128]{2,1,0:T(8,128)(2,1)S(1)} %all-to-all-done.1.p_ref, bf16[4,256,128]{2,1,0:T(8,128)(2,1)S(1)} %all_to_all.21.q0, ...), custom_call_target="tpu_custom_call" | custom-call | flops 2000000000 | bytes 2000000 | tf_op jit(solution)/shard_map/pallas_call | solution.py:76
  86.6 27.6 %all_to_all.22 = f32[64,16,128]{2,1,0:T(8,128)S(1)} all-to-all(f32[64,16,128]{2,1,0:T(8,128)S(1)} %bitcast.11), channel_id=1, replica_groups=mesh['aux_x'=4,'aux_y'=2,'aux_core'=2,'blk_y'=4,'blk_far'=4,'blk_near'=4..., dimensions={0} | all-to-all | bytes 1048576 | tf_op jit(solution)/shard_map/all_to_all | solution.py:111
  114.2 0.7 bitcast_reduce_fusion
  (1 shorter events, 0.0 us)
Async XLA Ops:
  46.2 25.0 %all-to-all-start.1 = ((bf16[4,256,128]{2,1,0:T(8,128)(2,1)}), bf16[4,256,128]{2,1,0:T(8,128)(2,1)S(1)}, u32[]{:S(2)}, u32[]{:S(2)}) async-start(bf16[4,256,128]{2,1,0:T(8,128)(2,1)} %broadcast_in_dim.7), calls=%async_computation.1 | async-start | bytes 524288 | tf_op jit(solution)/shard_map/all_to_all | solution.py:94
  52.1 27.5 %copy-start = (s32[1,64,64]{2,1,0:T(8,128)S(1)}, s32[1,64,64]{2,1,0:T(8,128)}, u32[]{:S(2)}) copy-start(s32[1,64,64]{2,1,0:T(8,128)} %param.7) | copy-start | bytes 49156
  52.1 27.4 %collective-permute-start.3 = (bf16[4,256,128]{2,1,0:T(8,128)(2,1)S(1)}, bf16[4,256,128]{2,1,0:T(8,128)(2,1)S(1)}, u32[]{:S(2)}, u32[]{:S(2)}) collective-permute-start(bf16[4,256,128]{2,1,0:T(8,128)(2,1)S(1)} %all_to_all.21.q0), channel_id=1, source_target_pairs={{0,1},{1,2},{2,3},{3,4},{4,5},{5,6},{6,7},{7,8},{8,9},{9,10},{10,1... | collective-permute-start | bytes 786440 | tf_op jit(solution)/shard_map/ppermute | solution.py:99
  60.2 19.4 %collective-permute-start = (bf16[4,256,128]{2,1,0:T(8,128)(2,1)S(1)}, bf16[4,256,128]{2,1,0:T(8,128)(2,1)S(1)}, u32[]{:S(2)}, u32[]{:S(2)}) collective-permute-start(bf16[4,256,128]{2,1,0:T(8,128)(2,1)S(1)} %all_to_all.21.q0), channel_id=1, source_target_pairs={{0,15},{1,0},{2,1},{3,2},{4,3},{5,4},{6,5},{7,6},{8,7},{9,8},{10,9... | collective-permute-start | bytes 786440 | tf_op jit(solution)/shard_map/ppermute | solution.py:99
  63.1 16.5 %copy-start.3 = (f32[1,128]{1,0:T(1,128)S(1)}, f32[1,128]{1,0:T(1,128)}, u32[]{:S(2)}) copy-start(f32[1,128]{1,0:T(1,128)} %virt.1) | copy-start | bytes 1540
  63.1 9.2 %collective-permute-start.2 = (bf16[2,256,128]{2,1,0:T(8,128)(2,1)S(1)}, bf16[2,256,128]{2,1,0:T(8,128)(2,1)S(1)}, u32[]{:S(2)}, u32[]{:S(2)}) collective-permute-start(bf16[2,256,128]{2,1,0:T(8,128)(2,1)S(1)} %get-tuple-element.5), channel_id=1, source_target_pairs={{0,2},{1,3},{2,4},{3,5},{4,6},{5,7},{6,8},{7,9},{8,10},{9,11},{10,... | collective-permute-start | bytes 393224 | tf_op jit(solution)/shard_map/ppermute | solution.py:99
  69.3 10.3 %collective-permute-start.1 = (bf16[2,256,128]{2,1,0:T(8,128)(2,1)S(1)}, bf16[2,256,128]{2,1,0:T(8,128)(2,1)S(1)}, u32[]{:S(2)}, u32[]{:S(2)}) collective-permute-start(bf16[2,256,128]{2,1,0:T(8,128)(2,1)S(1)} %get-tuple-element.6), channel_id=1, source_target_pairs={{0,14},{1,15},{2,0},{3,1},{4,2},{5,3},{6,4},{7,5},{8,6},{9,7},{10,... | collective-permute-start | bytes 393224 | tf_op jit(solution)/shard_map/ppermute | solution.py:99
  79.5 0.7 copy-start.1
  79.5 0.7 copy-start.2

commit v2 on v1

v2 whole, which is shorter than its diff:
```python
import functools

import jax
import jax.numpy as jnp
from jax import lax
from jax.experimental import pallas as pl
from jax.experimental.pallas import tpu as pltpu
from jax.sharding import Mesh, PartitionSpec as P

AUX = ("aux_x", "aux_y", "aux_core")
NP = 4
NZ = 16
EARLY = (5, -5, 1, 6, -4, -1, 4, -6)
LATE = (0, 2, 7, -3, -2, 3, -7, 8)
V = 128
AB = 128
NA = 256


def pair_kernel(shifts, finish, sig, keep, occ, virt, p_ref, *refs):
    counts = [ref.shape[0] for ref in refs if len(ref.shape) == 3 and ref.shape[1:] == (NA, V)]
    q_refs, refs = refs[: len(counts)], refs[len(counts) :]
    if finish:
        before, out, pcat, pcat_t, vb, acc = refs
    else:
        acc, pcat, pcat_t, vb = refs
    h = lax.axis_index("blk_y")
    w = lax.axis_index("blk_z")
    rows = lax.broadcasted_iota(jnp.int32, (NA, V), 0)
    zero = jnp.zeros((NA, V), jnp.bfloat16)

    def live(orbital):
        return jnp.where(rows < AB, sig[0, orbital], sig[1, orbital]) > 0

    p_index = [s * NZ + w for s in range(NP)]
    for s in range(NP):
        block = jnp.where(live(p_index[s]), p_ref[s], zero)
        pcat[:, s * V : (s + 1) * V] = block * 2
        pcat_t[s * V : (s + 1) * V, :] = block.T
    q_blocks = [ref.at[i] for ref, n in zip(q_refs, counts) for i in range(n)]
    q_index = [h * NZ + lax.rem(w + shift + NZ, NZ) for shift in shifts]
    va = virt[...]
    vb[...] = jnp.broadcast_to(va, (V, V)).T
    for c in range(0, len(shifts), 2):
        block = jnp.concatenate(
            [jnp.where(live(q_index[c + t]), q_blocks[c + t][...], zero) for t in range(2)], axis=1
        )
        twice = jnp.dot(block.T, pcat[...], preferred_element_type=jnp.float32)
        swapped = jnp.dot(pcat_t[...], block, preferred_element_type=jnp.float32)
        columns = []
        for s in range(NP):
            tiles = []
            for t in range(2):
                p, q = p_index[s], q_index[c + t]
                kept = keep[lax.min(p, q), lax.max(p, q)].astype(jnp.float32)
                total = occ[0, p] + occ[0, q]
                top = twice[t * V : (t + 1) * V, s * V : (s + 1) * V]
                top = top - swapped[s * V : (s + 1) * V, t * V : (t + 1) * V]
                tiles.append((kept * top / ((total - va) - vb[...])).astype(jnp.bfloat16))
            columns.append(jnp.concatenate(tiles, axis=0))
        tilde = jnp.concatenate(columns, axis=1)
        gamma = jnp.dot(block, tilde, preferred_element_type=jnp.float32)
        if c == 0:
            acc[...] = before[...] + gamma if finish else gamma
        else:
            acc[...] += gamma
    if finish:
        for s in range(NP):
            gamma = jnp.where(live(p_index[s]), acc[:, s * V : (s + 1) * V], 0.0)
            out[:, s] = gamma.reshape(16, 16, V)


def pair_terms(shifts, scalars, p_blocks, q_blocks, before=None):
    smem = pl.BlockSpec(memory_space=pltpu.SMEM)
    vmem = pl.BlockSpec(memory_space=pltpu.VMEM)
    sums = (NA, NP * V)
    arrays = [p_blocks, *q_blocks] + ([] if before is None else [before])
    return pl.pallas_call(
        functools.partial(pair_kernel, shifts, before is not None),
        out_shape=jax.ShapeDtypeStruct(sums if before is None else (16, NP, 16, V), jnp.float32),
        in_specs=[smem] * 3 + [vmem] * (1 + len(arrays)),
        out_specs=vmem,
        scratch_shapes=[
            pltpu.VMEM((NA, NP * V), jnp.bfloat16),
            pltpu.VMEM((NP * V, NA), jnp.bfloat16),
            pltpu.VMEM((V, V), jnp.float32),
        ]
        + ([] if before is None else [pltpu.VMEM(sums, jnp.float32)]),
        compiler_params=pltpu.CompilerParams(vmem_limit_bytes=24 * 2**20),
        cost_estimate=pl.CostEstimate(flops=10**9, bytes_accessed=2 * 10**6, transcendentals=5 * 10**5),
    )(*scalars, *arrays)


def ahead(x, shift):
    return lax.ppermute(x, "blk_z", [(i, (i - shift) % NZ) for i in range(NZ)])


def on_device(b_tensor, significance, pair_keep, occ_energy, virt_energy):
    own = lax.all_to_all(b_tensor[0], AUX, 0, 0, tiled=True).reshape(1, NA, V)
    up, down = ahead(own, 5), ahead(own, -5)
    p_blocks = lax.all_to_all(jnp.broadcast_to(own, (NP, NA, V)), "blk_y", 0, 0, tiled=True)
    three = jnp.concatenate([own, up, down], axis=0)
    scalars = (significance[:, 0, :].T, pair_keep[0], occ_energy.T, virt_energy)
    early = [up, down, ahead(three, 1), ahead(three, -1)]
    late = [own, ahead(three, 2), ahead(three, -2), ahead(up, 3)]
    part = pair_terms(EARLY, scalars, p_blocks, early)
    part = pair_terms(LATE, scalars, p_blocks, late, part)
    back = lax.all_to_all(part.reshape(64, 16, V), AUX + ("blk_y",), 0, 0, tiled=True)
    return back.reshape(16, NP, 16, V).sum(axis=1)[None]


def solution(mesh):
    fine = Mesh(mesh.devices.reshape(4, 2, 2, NP, NZ), AUX + ("blk_y", "blk_z"))
    blk = ("blk_y", "blk_z")
    return jax.shard_map(
        on_device,
        mesh=fine,
        in_specs=(
            P(blk, None, AUX, None),
            P(None, AUX, None),
            P(AUX, None, None),
            P(None, AUX),
            P(AUX, None),
        ),
        out_specs=P(blk, None, AUX, None),
        check_vma=False,
    )
```

time: 115 us -> 111 us (0.965)
  the two profiles are of different devices: /device:TPU:1 before, /device:TPU:65 now
where the time goes in v2:
time: 111 us; the launch traced here: 110 us
  starting transfers between devices  47.4 us (43%)
  blocking collectives  40.8 us (37%)
  waiting for transfers between devices  14.4 us (13%)
  Pallas kernels  5.08 us (5%)
  local copies, waits for them, and re-layouts  1.4 us (1%)
    ppermute x7, starting transfers between devices, ahead(): return lax.ppermute(x, 'blk_z', [(i, (i - shift) % NZ) for i in range(NZ)])  41.4 us
    all_to_all x1, blocking collectives, on_device(): lax.all_to_all(part.reshape(64, 16, V), AUX + ('blk_y',), 0, 0, tiled=True)  29 us
    ppermute x7, waiting for transfers between devices, ahead(): return lax.ppermute(x, 'blk_z', [(i, (i - shift) % NZ) for i in range(NZ)])  14.4 us
    all_to_all x1, blocking collectives, on_device(): own = lax.all_to_all(b_tensor[0], AUX, 0, 0, tiled=True).reshape(1, NA, V)  11.8 us
    all_to_all x1, starting transfers between devices, on_device(): lax.all_to_all(jnp.broadcast_to(own, (NP, NA, V)), 'blk_y', 0, 0, tiled=T...  5.91 us
    pallas_call x2, Pallas kernels, pair_terms(): pl.pallas_call(functools.partial(pair_kernel, shifts, before is not None)...  5.08 us
  transfers between devices with their start and end apart: 8, of which 2 were waited for; matrix products, arithmetic and copies ran while one was open for 0% of the time, Pallas kernels for 2%

profile of v2, /device:TPU:65, one launch (start us, length us, event | category | flops | bytes accessed | tf_op | source)
XLA Modules:
  0.0 110.0 jit_solution(9598193590087985820)
XLA Ops:
  0.0 11.8 %all_to_all.15 = bf16[16,16,128]{2,1,0:T(8,128)(2,1)S(1)} all-to-all(bf16[16,16,128]{2,1,0:T(8,128)(2,1)} %bitcast.24), channel_id=1, replica_groups=mesh['aux_x'=4,'aux_y'=2,'aux_core'=2,'blk_y'=4,'blk_z'=16] {'aux_x','au..., dimensions={0} | all-to-all | bytes 131072 | tf_op jit(solution)/shard_map/all_to_all | solution.py:99
  11.8 0.7 broadcast_in_dim.11
  12.6 5.9 %all-to-all-start.1 = ((bf16[4,256,128]{2,1,0:T(8,128)(2,1)}), bf16[4,256,128]{2,1,0:T(8,128)(2,1)S(1)}, u32[]{:S(2)}, u32[]{:S(2)}) async-start(bf16[4,256,128]{2,1,0:T(8,128)(2,1)} %broadcast_in_dim.11), calls=%async_computation.1 | async-start | bytes 524288 | tf_op jit(solution)/shard_map/all_to_all | solution.py:101
  18.5 0.0 copy-start
  18.5 12.6 %collective-permute-start.1 = (bf16[1,256,128]{2,1,0:T(8,128)(2,1)S(1)}, bf16[1,256,128]{2,1,0:T(8,128)(2,1)S(1)}, u32[]{:S(2)}, u32[]{:S(2)}) collective-permute-start(bf16[1,256,128]{2,1,0:T(8,128)(2,1)S(1)} %bitcast.13), channel_id=1, source_target_pairs={{0,5},{1,6},{2,7},{3,8},{4,9},{5,10},{6,11},{7,12},{8,13},{9,14},{... | collective-permute-start | bytes 196616 | tf_op jit(solution)/shard_map/ppermute | solution.py:95
  31.1 6.5 %collective-permute-start = (bf16[1,256,128]{2,1,0:T(8,128)(2,1)S(1)}, bf16[1,256,128]{2,1,0:T(8,128)(2,1)S(1)}, u32[]{:S(2)}, u32[]{:S(2)}) collective-permute-start(bf16[1,256,128]{2,1,0:T(8,128)(2,1)S(1)} %bitcast.14), channel_id=1, source_target_pairs={{0,11},{1,12},{2,13},{3,14},{4,15},{5,0},{6,1},{7,2},{8,3},{9,4},{... | collective-permute-start | bytes 196616 | tf_op jit(solution)/shard_map/ppermute | solution.py:95
  37.5 0.0 collective-permute-done.1.refs_1_
  37.5 5.0 %collective-permute-done.refs_0_ = bf16[1,256,128]{2,1,0:T(8,128)(2,1)S(1)} collective-permute-done((bf16[1,256,128]{2,1,0:T(8,128)(2,1)S(1)}, bf16[1,256,128]{2,1,0:T(8,128)(2,1)S(1)}, u32[]{:S(2)}, u32[]{:S(2)}) %collective-permute-start) | collective-permute-done | bytes 65568 | tf_op jit(solution)/shard_map/ppermute | solution.py:95
  42.6 0.0 copy-start.3
  42.6 3.1 %collective-permute-start.6 = (bf16[3,256,128]{2,1,0:T(8,128)(2,1)S(1)}, bf16[3,256,128]{2,1,0:T(8,128)(2,1)S(1)}, u32[]{:S(2)}, u32[]{:S(2)}) collective-permute-start(bf16[3,256,128]{2,1,0:T(8,128)(2,1)S(1)} %pad_maximum_fusion), channel_id=1, source_target_pairs={{0,1},{1,2},{2,3},{3,4},{4,5},{5,6},{6,7},{7,8},{8,9},{9,10},{10,1... | collective-permute-start | bytes 589832 | tf_op jit(solution)/shard_map/ppermute | solution.py:95
  45.7 2.2 %collective-permute-start.5 = (bf16[3,256,128]{2,1,0:T(8,128)(2,1)S(1)}, bf16[3,256,128]{2,1,0:T(8,128)(2,1)S(1)}, u32[]{:S(2)}, u32[]{:S(2)}) collective-permute-start(bf16[3,256,128]{2,1,0:T(8,128)(2,1)S(1)} %pad_maximum_fusion), channel_id=1, source_target_pairs={{0,15},{1,0},{2,1},{3,2},{4,3},{5,4},{6,5},{7,6},{8,7},{9,8},{10,9... | collective-permute-start | bytes 589832 | tf_op jit(solution)/shard_map/ppermute | solution.py:95
  47.9 11.9 %collective-permute-start.3 = (bf16[3,256,128]{2,1,0:T(8,128)(2,1)S(1)}, bf16[3,256,128]{2,1,0:T(8,128)(2,1)S(1)}, u32[]{:S(2)}, u32[]{:S(2)}) collective-permute-start(bf16[3,256,128]{2,1,0:T(8,128)(2,1)S(1)} %pad_maximum_fusion), channel_id=1, source_target_pairs={{0,2},{1,3},{2,4},{3,5},{4,6},{5,7},{6,8},{7,9},{8,10},{9,11},{10,... | collective-permute-start | bytes 589832 | tf_op jit(solution)/shard_map/ppermute | solution.py:95
  59.8 1.9 %collective-permute-start.2 = (bf16[3,256,128]{2,1,0:T(8,128)(2,1)S(1)}, bf16[3,256,128]{2,1,0:T(8,128)(2,1)S(1)}, u32[]{:S(2)}, u32[]{:S(2)}) collective-permute-start(bf16[3,256,128]{2,1,0:T(8,128)(2,1)S(1)} %pad_maximum_fusion), channel_id=1, source_target_pairs={{0,14},{1,15},{2,0},{3,1},{4,2},{5,3},{6,4},{7,5},{8,6},{9,7},{10,... | collective-permute-start | bytes 589832 | tf_op jit(solution)/shard_map/ppermute | solution.py:95
  61.7 3.3 %collective-permute-start.4 = (bf16[1,256,128]{2,1,0:T(8,128)(2,1)S(1)}, bf16[1,256,128]{2,1,0:T(8,128)(2,1)S(1)}, u32[]{:S(2)}, u32[]{:S(2)}) collective-permute-start(bf16[1,256,128]{2,1,0:T(8,128)(2,1)S(1)} %collective-permute-done.refs_0_), channel_id=1, source_target_pairs={{0,13},{1,14},{2,15},{3,0},{4,1},{5,2},{6,3},{7,4},{8,5},{9,6},{10... | collective-permute-start | bytes 196616 | tf_op jit(solution)/shard_map/ppermute | solution.py:95
  65.1 0.0 collective-permute-done.6.refs_3_
  65.1 0.0 collective-permute-done.5.refs_2_
  65.1 0.0 all-to-all-done.1.p_ref
  65.1 0.0 copy-start.1
  65.1 0.0 copy-start.2
  65.1 0.0 copy-done
  65.1 0.0 copy-done.3
  65.1 0.6 copy-done.1
  65.8 0.0 copy-done.2
  65.8 2.5 %shard_map.55.refs_4_ = f32[256,512]{1,0:T(8,128)S(1)} custom-call(s32[2,64]{1,0:T(2,128)S(1)} %bitcast.20, s32[64,64]{1,0:T(8,128)S(1)} %bitcast.18, f32[1,64]{1,0:T(1,128)S(1)} %bitcast.22, f32[1,128]{1,0:T(1,128)S(1)} %copy-done.3, bf16[4,256,128]{2,1,0:T(8,128)(2,1)S(1)} %all-to-all-done.1.p_ref, bf16[1,256,128]{2,1,0:T(8,128)(2,1)S(1)} %collective-permute-done.refs_0_, ...), custom_call_target="tpu_custom_call" | custom-call | flops 1000000000 | bytes 2000000 | tf_op jit(solution)/shard_map/pallas_call | solution.py:78
  68.3 9.4 %collective-permute-done.4.refs_3_ = bf16[1,256,128]{2,1,0:T(8,128)(2,1)S(1)} collective-permute-done((bf16[1,256,128]{2,1,0:T(8,128)(2,1)S(1)}, bf16[1,256,128]{2,1,0:T(8,128)(2,1)S(1)}, u32[]{:S(2)}, u32[]{:S(2)}) %collective-permute-start.4) | collective-permute-done | bytes 65568 | tf_op jit(solution)/shard_map/ppermute | solution.py:95
  77.7 0.0 collective-permute-done.3.refs_2_
  77.7 0.0 collective-permute-done.2.refs_1_
  77.7 2.5 %shard_map.56 = f32[16,4,16,128]{3,2,1,0:T(8,128)S(1)} custom-call(s32[2,64]{1,0:T(2,128)S(1)} %bitcast.21, s32[64,64]{1,0:T(8,128)S(1)} %bitcast.19, f32[1,64]{1,0:T(1,128)S(1)} %bitcast.23, f32[1,128]{1,0:T(1,128)S(1)} %copy-done.3, bf16[4,256,128]{2,1,0:T(8,128)(2,1)S(1)} %all-to-all-done.1.p_ref, bf16[1,256,128]{2,1,0:T(8,128)(2,1)S(1)} %bitcast.16, ...), custom_call_target="tpu_custom_call" | custom-call | flops 1000000000 | bytes 2000000 | tf_op jit(solution)/shard_map/pallas_call | solution.py:78
  80.3 29.0 %all_to_all.16 = f32[64,16,128]{2,1,0:T(8,128)S(1)} all-to-all(f32[64,16,128]{2,1,0:T(8,128)S(1)} %bitcast.17), channel_id=1, replica_groups=mesh['aux_x'=4,'aux_y'=2,'aux_core'=2,'blk_y'=4,'blk_z'=16] {'aux_x','au..., dimensions={0} | all-to-all | bytes 1048576 | tf_op jit(solution)/shard_map/all_to_all | solution.py:108
  109.3 0.7 bitcast_reduce_fusion
  (1 shorter events, 0.0 us)
Async XLA Ops:
  12.6 52.5 %all-to-all-start.1 = ((bf16[4,256,128]{2,1,0:T(8,128)(2,1)}), bf16[4,256,128]{2,1,0:T(8,128)(2,1)S(1)}, u32[]{:S(2)}, u32[]{:S(2)}) async-start(bf16[4,256,128]{2,1,0:T(8,128)(2,1)} %broadcast_in_dim.11), calls=%async_computation.1 | async-start | bytes 524288 | tf_op jit(solution)/shard_map/all_to_all | solution.py:101
  18.5 46.6 %copy-start = (s32[1,64,64]{2,1,0:T(8,128)S(1)}, s32[1,64,64]{2,1,0:T(8,128)}, u32[]{:S(2)}) copy-start(s32[1,64,64]{2,1,0:T(8,128)} %param.7) | copy-start | bytes 49156
  18.5 19.1 %collective-permute-start.1 = (bf16[1,256,128]{2,1,0:T(8,128)(2,1)S(1)}, bf16[1,256,128]{2,1,0:T(8,128)(2,1)S(1)}, u32[]{:S(2)}, u32[]{:S(2)}) collective-permute-start(bf16[1,256,128]{2,1,0:T(8,128)(2,1)S(1)} %bitcast.13), channel_id=1, source_target_pairs={{0,5},{1,6},{2,7},{3,8},{4,9},{5,10},{6,11},{7,12},{8,13},{9,14},{... | collective-permute-start | bytes 196616 | tf_op jit(solution)/shard_map/ppermute | solution.py:95
  31.1 11.5 %collective-permute-start = (bf16[1,256,128]{2,1,0:T(8,128)(2,1)S(1)}, bf16[1,256,128]{2,1,0:T(8,128)(2,1)S(1)}, u32[]{:S(2)}, u32[]{:S(2)}) collective-permute-start(bf16[1,256,128]{2,1,0:T(8,128)(2,1)S(1)} %bitcast.14), channel_id=1, source_target_pairs={{0,11},{1,12},{2,13},{3,14},{4,15},{5,0},{6,1},{7,2},{8,3},{9,4},{... | collective-permute-start | bytes 196616 | tf_op jit(solution)/shard_map/ppermute | solution.py:95
  42.6 22.5 %copy-start.3 = (f32[1,128]{1,0:T(1,128)S(1)}, f32[1,128]{1,0:T(1,128)}, u32[]{:S(2)}) copy-start(f32[1,128]{1,0:T(1,128)} %virt.3) | copy-start | bytes 1540
  42.6 22.4 %collective-permute-start.6 = (bf16[3,256,128]{2,1,0:T(8,128)(2,1)S(1)}, bf16[3,256,128]{2,1,0:T(8,128)(2,1)S(1)}, u32[]{:S(2)}, u32[]{:S(2)}) collective-permute-start(bf16[3,256,128]{2,1,0:T(8,128)(2,1)S(1)} %pad_maximum_fusion), channel_id=1, source_target_pairs={{0,1},{1,2},{2,3},{3,4},{4,5},{5,6},{6,7},{7,8},{8,9},{9,10},{10,1... | collective-permute-start | bytes 589832 | tf_op jit(solution)/shard_map/ppermute | solution.py:95
  45.7 19.3 %collective-permute-start.5 = (bf16[3,256,128]{2,1,0:T(8,128)(2,1)S(1)}, bf16[3,256,128]{2,1,0:T(8,128)(2,1)S(1)}, u32[]{:S(2)}, u32[]{:S(2)}) collective-permute-start(bf16[3,256,128]{2,1,0:T(8,128)(2,1)S(1)} %pad_maximum_fusion), channel_id=1, source_target_pairs={{0,15},{1,0},{2,1},{3,2},{4,3},{5,4},{6,5},{7,6},{8,7},{9,8},{10,9... | collective-permute-start | bytes 589832 | tf_op jit(solution)/shard_map/ppermute | solution.py:95
  47.9 29.8 %collective-permute-start.3 = (bf16[3,256,128]{2,1,0:T(8,128)(2,1)S(1)}, bf16[3,256,128]{2,1,0:T(8,128)(2,1)S(1)}, u32[]{:S(2)}, u32[]{:S(2)}) collective-permute-start(bf16[3,256,128]{2,1,0:T(8,128)(2,1)S(1)} %pad_maximum_fusion), channel_id=1, source_target_pairs={{0,2},{1,3},{2,4},{3,5},{4,6},{5,7},{6,8},{7,9},{8,10},{9,11},{10,... | collective-permute-start | bytes 589832 | tf_op jit(solution)/shard_map/ppermute | solution.py:95
  59.8 17.9 %collective-permute-start.2 = (bf16[3,256,128]{2,1,0:T(8,128)(2,1)S(1)}, bf16[3,256,128]{2,1,0:T(8,128)(2,1)S(1)}, u32[]{:S(2)}, u32[]{:S(2)}) collective-permute-start(bf16[3,256,128]{2,1,0:T(8,128)(2,1)S(1)} %pad_maximum_fusion), channel_id=1, source_target_pairs={{0,14},{1,15},{2,0},{3,1},{4,2},{5,3},{6,4},{7,5},{8,6},{9,7},{10,... | collective-permute-start | bytes 589832 | tf_op jit(solution)/shard_map/ppermute | solution.py:95
  61.7 16.0 %collective-permute-start.4 = (bf16[1,256,128]{2,1,0:T(8,128)(2,1)S(1)}, bf16[1,256,128]{2,1,0:T(8,128)(2,1)S(1)}, u32[]{:S(2)}, u32[]{:S(2)}) collective-permute-start(bf16[1,256,128]{2,1,0:T(8,128)(2,1)S(1)} %collective-permute-done.refs_0_), channel_id=1, source_target_pairs={{0,13},{1,14},{2,15},{3,0},{4,1},{5,2},{6,3},{7,4},{8,5},{9,6},{10... | collective-permute-start | bytes 196616 | tf_op jit(solution)/shard_map/ppermute | solution.py:95
  65.1 0.7 copy-start.1
  65.1 0.7 copy-start.2

commit v3 on v2

--- a/solution.py
+++ b/solution.py
@@ -10,14 +10,13 @@
 AUX = ("aux_x", "aux_y", "aux_core")
 NP = 4
 NZ = 16
-EARLY = (5, -5, 1, 6, -4, -1, 4, -6)
-LATE = (0, 2, 7, -3, -2, 3, -7, 8)
+NF = NZ // 2
 V = 128
 AB = 128
 NA = 256
 
 
-def pair_kernel(shifts, finish, sig, keep, occ, virt, p_ref, *refs):
+def pair_kernel(parity, finish, sig, keep, occ, virt, p_ref, *refs):
     counts = [ref.shape[0] for ref in refs if len(ref.shape) == 3 and ref.shape[1:] == (NA, V)]
     q_refs, refs = refs[: len(counts)], refs[len(counts) :]
     if finish:
@@ -25,7 +24,8 @@
     else:
         acc, pcat, pcat_t, vb = refs
     h = lax.axis_index("blk_y")
-    w = lax.axis_index("blk_z")
+    near = lax.axis_index("blk_near")
+    w = 2 * lax.axis_index("blk_far") + near
     rows = lax.broadcasted_iota(jnp.int32, (NA, V), 0)
     zero = jnp.zeros((NA, V), jnp.bfloat16)
 
@@ -38,10 +38,11 @@
         pcat[:, s * V : (s + 1) * V] = block * 2
         pcat_t[s * V : (s + 1) * V, :] = block.T
     q_blocks = [ref.at[i] for ref, n in zip(q_refs, counts) for i in range(n)]
-    q_index = [h * NZ + lax.rem(w + shift + NZ, NZ) for shift in shifts]
+    near = near if parity == 0 else 1 - near
+    q_index = [h * NZ + 2 * far + near for far in range(NF)]
     va = virt[...]
     vb[...] = jnp.broadcast_to(va, (V, V)).T
-    for c in range(0, len(shifts), 2):
+    for c in range(0, NF, 2):
         block = jnp.concatenate(
             [jnp.where(live(q_index[c + t]), q_blocks[c + t][...], zero) for t in range(2)], axis=1
         )
@@ -70,13 +71,13 @@
             out[:, s] = gamma.reshape(16, 16, V)
 
 
-def pair_terms(shifts, scalars, p_blocks, q_blocks, before=None):
+def pair_terms(parity, scalars, p_blocks, q_blocks, before=None):
     smem = pl.BlockSpec(memory_space=pltpu.SMEM)
     vmem = pl.BlockSpec(memory_space=pltpu.VMEM)
     sums = (NA, NP * V)
     arrays = [p_blocks, *q_blocks] + ([] if before is None else [before])
     return pl.pallas_call(
-        functools.partial(pair_kernel, shifts, before is not None),
+        functools.partial(pair_kernel, parity, before is not None),
         out_shape=jax.ShapeDtypeStruct(sums if before is None else (16, NP, 16, V), jnp.float32),
         in_specs=[smem] * 3 + [vmem] * (1 + len(arrays)),
         out_specs=vmem,
@@ -92,26 +93,24 @@
 
 
 def ahead(x, shift):
-    return lax.ppermute(x, "blk_z", [(i, (i - shift) % NZ) for i in range(NZ)])
+    return lax.ppermute(x, ("blk_far", "blk_near"), [(i, (i - shift) % NZ) for i in range(NZ)])
 
 
 def on_device(b_tensor, significance, pair_keep, occ_energy, virt_energy):
     own = lax.all_to_all(b_tensor[0], AUX, 0, 0, tiled=True).reshape(1, NA, V)
-    up, down = ahead(own, 5), ahead(own, -5)
     p_blocks = lax.all_to_all(jnp.broadcast_to(own, (NP, NA, V)), "blk_y", 0, 0, tiled=True)
-    three = jnp.concatenate([own, up, down], axis=0)
+    same = lax.all_gather(own, "blk_far", axis=0, tiled=True)
+    other = [ahead(same[: NF // 2], 1), ahead(same[NF // 2 :], -1)]
     scalars = (significance[:, 0, :].T, pair_keep[0], occ_energy.T, virt_energy)
-    early = [up, down, ahead(three, 1), ahead(three, -1)]
-    late = [own, ahead(three, 2), ahead(three, -2), ahead(up, 3)]
-    part = pair_terms(EARLY, scalars, p_blocks, early)
-    part = pair_terms(LATE, scalars, p_blocks, late, part)
+    part = pair_terms(0, scalars, p_blocks, [same])
+    part = pair_terms(1, scalars, p_blocks, other, part)
     back = lax.all_to_all(part.reshape(64, 16, V), AUX + ("blk_y",), 0, 0, tiled=True)
     return back.reshape(16, NP, 16, V).sum(axis=1)[None]
 
 
 def solution(mesh):
-    fine = Mesh(mesh.devices.reshape(4, 2, 2, NP, NZ), AUX + ("blk_y", "blk_z"))
-    blk = ("blk_y", "blk_z")
+    blk = ("blk_y", "blk_far", "blk_near")
+    fine = Mesh(mesh.devices.reshape(4, 2, 2, NP, NF, 2), AUX + blk)
     return jax.shard_map(
         on_device,
         mesh=fine,

time: 111 us -> 108 us (0.973)
  the two profiles are of different devices: /device:TPU:65 before, /device:TPU:1 now
where the time goes in v3:
time: 108 us
  blocking collectives  86.5 us (80%)
  starting transfers between devices  10.9 us (10%)
  Pallas kernels  5.08 us (5%)
  waiting for transfers between devices  3.15 us (3%)
  local copies, waits for them, and re-layouts  1.43 us (1%)
    all_to_all x1, blocking collectives, on_device(): lax.all_to_all(part.reshape(64, 16, V), AUX + ('blk_y',), 0, 0, tiled=True)  35 us
    all_gather x1, blocking collectives, on_device(): same = lax.all_gather(own, 'blk_far', axis=0, tiled=True)  28.1 us
    all_to_all x1, blocking collectives, on_device(): own = lax.all_to_all(b_tensor[0], AUX, 0, 0, tiled=True).reshape(1, NA, V)  23.3 us
    ppermute x2, starting transfers between devices, ahead(): lax.ppermute(x, ('blk_far', 'blk_near'), [(i, (i - shift) % NZ) for i in...  7.45 us
    pallas_call x2, Pallas kernels, pair_terms(): pl.pallas_call(functools.partial(pair_kernel, parity, before is not None)...  5.08 us
    all_to_all x1, starting transfers between devices, on_device(): lax.all_to_all(jnp.broadcast_to(own, (NP, NA, V)), 'blk_y', 0, 0, tiled=T...  3.4 us
    ppermute x2, waiting for transfers between devices, ahead(): lax.ppermute(x, ('blk_far', 'blk_near'), [(i, (i - shift) % NZ) for i in...  3.15 us
  transfers between devices with their start and end apart: 3, of which 1 were waited for; matrix products, arithmetic and copies ran while one was open for 0% of the time, Pallas kernels for 2%

profile of v3, /device:TPU:1, one launch (start us, length us, event | category | flops | bytes accessed | tf_op | source)
XLA Modules:
  0.0 107.8 jit_solution(3943035114873188218)
XLA Ops:
  0.0 23.3 %all_to_all.15 = bf16[16,16,128]{2,1,0:T(8,128)(2,1)S(1)} all-to-all(bf16[16,16,128]{2,1,0:T(8,128)(2,1)} %bitcast.21), channel_id=1, replica_groups=mesh['aux_x'=4,'aux_y'=2,'aux_core'=2,'blk_y'=4,'blk_far'=8,'blk_near'=2..., dimensions={0} | all-to-all | bytes 131072 | tf_op jit(solution)/shard_map/all_to_all | solution.py:100
  23.3 0.7 broadcast_in_dim.11
  24.0 3.4 %all-to-all-start.1 = ((bf16[4,256,128]{2,1,0:T(8,128)(2,1)}), bf16[4,256,128]{2,1,0:T(8,128)(2,1)S(1)}, u32[]{:S(2)}, u32[]{:S(2)}) async-start(bf16[4,256,128]{2,1,0:T(8,128)(2,1)} %broadcast_in_dim.11), calls=%async_computation.1 | async-start | bytes 524288 | tf_op jit(solution)/shard_map/all_to_all | solution.py:101
  27.5 28.1 %all_gather.3.refs_0_ = bf16[8,256,128]{2,1,0:T(8,128)(2,1)S(1)} all-gather(bf16[1,256,128]{2,1,0:T(8,128)(2,1)S(1)} %bitcast.20), channel_id=1, replica_groups=mesh['aux_x'=4,'aux_y'=2,'aux_core'=2,'blk_y'=4,'blk_far'=8,'blk_near'=2..., dimensions={0}, use_global_device_ids=true | all-gather | bytes 589824 | tf_op jit(solution)/shard_map/all_gather | solution.py:102
  55.6 0.0 copy-start
  55.6 0.0 copy-start.3
  55.6 5.5 %collective-permute-start = (bf16[4,256,128]{2,1,0:T(8,128)(2,1)S(1)}, bf16[4,256,128]{2,1,0:T(8,128)(2,1)S(1)}, u32[]{:S(2)}, u32[]{:S(2)}) collective-permute-start(bf16[4,256,128]{2,1,0:T(8,128)(2,1)S(1)} %get-tuple-element.6), channel_id=1, source_target_pairs={{0,15},{1,0},{2,1},{3,2},{4,3},{5,4},{6,5},{7,6},{8,7},{9,8},{10,9... | collective-permute-start | bytes 786440 | tf_op jit(solution)/shard_map/ppermute | solution.py:96
  61.2 1.9 %collective-permute-start.1 = (bf16[4,256,128]{2,1,0:T(8,128)(2,1)S(1)}, bf16[4,256,128]{2,1,0:T(8,128)(2,1)S(1)}, u32[]{:S(2)}, u32[]{:S(2)}) collective-permute-start(bf16[4,256,128]{2,1,0:T(8,128)(2,1)S(1)} %get-tuple-element.5), channel_id=1, source_target_pairs={{0,1},{1,2},{2,3},{3,4},{4,5},{5,6},{6,7},{7,8},{8,9},{9,10},{10,1... | collective-permute-start | bytes 786440 | tf_op jit(solution)/shard_map/ppermute | solution.py:96
  63.1 0.0 all-to-all-done.1.p_ref
  63.1 0.0 copy-start.1
  63.1 0.0 copy-start.2
  63.1 0.0 copy-done
  63.2 0.0 copy-done.3
  63.2 0.6 copy-done.1
  63.8 0.0 copy-done.2
  63.8 2.5 %shard_map.55.refs_2_ = f32[256,512]{1,0:T(8,128)S(1)} custom-call(s32[2,64]{1,0:T(2,128)S(1)} %bitcast.15, s32[64,64]{1,0:T(8,128)S(1)} %bitcast.13, f32[1,64]{1,0:T(1,128)S(1)} %bitcast.17, f32[1,128]{1,0:T(1,128)S(1)} %copy-done.3, bf16[4,256,128]{2,1,0:T(8,128)(2,1)S(1)} %all-to-all-done.1.p_ref, bf16[8,256,128]{2,1,0:T(8,128)(2,1)S(1)} %all_gather.3.refs_0_), custom_call_target="tpu_custom_call" | custom-call | flops 1000000000 | bytes 2000000 | tf_op jit(solution)/shard_map/pallas_call | solution.py:79
  66.3 0.0 collective-permute-done.refs_0_
  66.4 3.1 %collective-permute-done.1.refs_1_ = bf16[4,256,128]{2,1,0:T(8,128)(2,1)S(1)} collective-permute-done((bf16[4,256,128]{2,1,0:T(8,128)(2,1)S(1)}, bf16[4,256,128]{2,1,0:T(8,128)(2,1)S(1)}, u32[]{:S(2)}, u32[]{:S(2)}) %collective-permute-start.1) | collective-permute-done | bytes 262176 | tf_op jit(solution)/shard_map/ppermute | solution.py:96
  69.5 2.5 %shard_map.56 = f32[16,4,16,128]{3,2,1,0:T(8,128)S(1)} custom-call(s32[2,64]{1,0:T(2,128)S(1)} %bitcast.16, s32[64,64]{1,0:T(8,128)S(1)} %bitcast.14, f32[1,64]{1,0:T(1,128)S(1)} %bitcast.18, f32[1,128]{1,0:T(1,128)S(1)} %copy-done.3, bf16[4,256,128]{2,1,0:T(8,128)(2,1)S(1)} %all-to-all-done.1.p_ref, bf16[4,256,128]{2,1,0:T(8,128)(2,1)S(1)} %collective-permute-done.refs_0_, ...), custom_call_target="tpu_custom_call" | custom-call | flops 1000000000 | bytes 2000000 | tf_op jit(solution)/shard_map/pallas_call | solution.py:79
  72.1 35.0 %all_to_all.16 = f32[64,16,128]{2,1,0:T(8,128)S(1)} all-to-all(f32[64,16,128]{2,1,0:T(8,128)S(1)} %bitcast.12), channel_id=1, replica_groups=mesh['aux_x'=4,'aux_y'=2,'aux_core'=2,'blk_y'=4,'blk_far'=8,'blk_near'=2..., dimensions={0} | all-to-all | bytes 1048576 | tf_op jit(solution)/shard_map/all_to_all | solution.py:107
  107.1 0.7 bitcast_reduce_fusion
  (1 shorter events, 0.0 us)
Async XLA Ops:
  24.0 39.1 %all-to-all-start.1 = ((bf16[4,256,128]{2,1,0:T(8,128)(2,1)}), bf16[4,256,128]{2,1,0:T(8,128)(2,1)S(1)}, u32[]{:S(2)}, u32[]{:S(2)}) async-start(bf16[4,256,128]{2,1,0:T(8,128)(2,1)} %broadcast_in_dim.11), calls=%async_computation.1 | async-start | bytes 524288 | tf_op jit(solution)/shard_map/all_to_all | solution.py:101
  55.6 7.6 %copy-start = (s32[1,64,64]{2,1,0:T(8,128)S(1)}, s32[1,64,64]{2,1,0:T(8,128)}, u32[]{:S(2)}) copy-start(s32[1,64,64]{2,1,0:T(8,128)} %param.7) | copy-start | bytes 49156
  55.6 7.6 %copy-start.3 = (f32[1,128]{1,0:T(1,128)S(1)}, f32[1,128]{1,0:T(1,128)}, u32[]{:S(2)}) copy-start(f32[1,128]{1,0:T(1,128)} %virt.3) | copy-start | bytes 1540
  55.6 10.7 %collective-permute-start = (bf16[4,256,128]{2,1,0:T(8,128)(2,1)S(1)}, bf16[4,256,128]{2,1,0:T(8,128)(2,1)S(1)}, u32[]{:S(2)}, u32[]{:S(2)}) collective-permute-start(bf16[4,256,128]{2,1,0:T(8,128)(2,1)S(1)} %get-tuple-element.6), channel_id=1, source_target_pairs={{0,15},{1,0},{2,1},{3,2},{4,3},{5,4},{6,5},{7,6},{8,7},{9,8},{10,9... | collective-permute-start | bytes 786440 | tf_op jit(solution)/shard_map/ppermute | solution.py:96
  61.2 8.3 %collective-permute-start.1 = (bf16[4,256,128]{2,1,0:T(8,128)(2,1)S(1)}, bf16[4,256,128]{2,1,0:T(8,128)(2,1)S(1)}, u32[]{:S(2)}, u32[]{:S(2)}) collective-permute-start(bf16[4,256,128]{2,1,0:T(8,128)(2,1)S(1)} %get-tuple-element.5), channel_id=1, source_target_pairs={{0,1},{1,2},{2,3},{3,4},{4,5},{5,6},{6,7},{7,8},{8,9},{9,10},{10,1... | collective-permute-start | bytes 786440 | tf_op jit(solution)/shard_map/ppermute | solution.py:96
  63.1 0.7 copy-start.1
  63.1 0.7 copy-start.2

commit v4 on v3

--- a/solution.py
+++ b/solution.py
@@ -68,7 +68,7 @@
     if finish:
         for s in range(NP):
             gamma = jnp.where(live(p_index[s]), acc[:, s * V : (s + 1) * V], 0.0)
-            out[:, s] = gamma.reshape(16, 16, V)
+            out[s] = gamma.reshape(16, 16, V)
 
 
 def pair_terms(parity, scalars, p_blocks, q_blocks, before=None):
@@ -78,7 +78,7 @@
     arrays = [p_blocks, *q_blocks] + ([] if before is None else [before])
     return pl.pallas_call(
         functools.partial(pair_kernel, parity, before is not None),
-        out_shape=jax.ShapeDtypeStruct(sums if before is None else (16, NP, 16, V), jnp.float32),
+        out_shape=jax.ShapeDtypeStruct(sums if before is None else (NP, 16, 16, V), jnp.float32),
         in_specs=[smem] * 3 + [vmem] * (1 + len(arrays)),
         out_specs=vmem,
         scratch_shapes=[
@@ -98,14 +98,15 @@
 
 def on_device(b_tensor, significance, pair_keep, occ_energy, virt_energy):
     own = lax.all_to_all(b_tensor[0], AUX, 0, 0, tiled=True).reshape(1, NA, V)
+    same = lax.all_gather(own, "blk_far", axis=0, tiled=True)
+    own, same = lax.optimization_barrier((own, same))
     p_blocks = lax.all_to_all(jnp.broadcast_to(own, (NP, NA, V)), "blk_y", 0, 0, tiled=True)
-    same = lax.all_gather(own, "blk_far", axis=0, tiled=True)
     other = [ahead(same[: NF // 2], 1), ahead(same[NF // 2 :], -1)]
     scalars = (significance[:, 0, :].T, pair_keep[0], occ_energy.T, virt_energy)
     part = pair_terms(0, scalars, p_blocks, [same])
     part = pair_terms(1, scalars, p_blocks, other, part)
-    back = lax.all_to_all(part.reshape(64, 16, V), AUX + ("blk_y",), 0, 0, tiled=True)
-    return back.reshape(16, NP, 16, V).sum(axis=1)[None]
+    back = lax.all_to_all(part.reshape(64, 16, V), ("blk_y",) + AUX, 0, 0, tiled=True)
+    return back.reshape(NP, 16, 16, V).sum(axis=0)[None]
 
 
 def solution(mesh):

time: 108 us -> 106 us (0.981)
  blocking collectives: 86.5 us -> 82.3 us
  starting transfers between devices: 10.9 us -> 13 us
    all_to_all x1, starting transfers between devices: 3.4 us -> 5.91 us  [on_device(): lax.all_to_all(jnp.broadcast_to(own, (NP, NA, V)), 'blk_y', 0, 0, tiled=T...]
    all_gather x1, blocking collectives: 28.1 us -> 26 us  [on_device(): same = lax.all_gather(own, 'blk_far', axis=0, tiled=True)]
    all_to_all x1, blocking collectives: 35 us -> 33 us  [on_device(): lax.all_to_all(part.reshape(64, 16, V), ('blk_y',) + AUX, 0, 0, tiled=True)]
  transfers between devices with their start and end apart: 3 -> 3, of which waited for: 1 -> 2; matrix products, arithmetic and copies ran while one was open for 0% -> 0% of each run, Pallas kernels for 2% -> 2%
where the time goes in v4:
time: 106 us
  blocking collectives  82.3 us (78%)
  starting transfers between devices  13 us (12%)
  Pallas kernels  5.08 us (5%)
  waiting for transfers between devices  3.46 us (3%)
  local copies, waits for them, and re-layouts  1.45 us (1%)
    all_to_all x1, blocking collectives, on_device(): lax.all_to_all(part.reshape(64, 16, V), ('blk_y',) + AUX, 0, 0, tiled=True)  33 us
    all_gather x1, blocking collectives, on_device(): same = lax.all_gather(own, 'blk_far', axis=0, tiled=True)  26 us
    all_to_all x1, blocking collectives, on_device(): own = lax.all_to_all(b_tensor[0], AUX, 0, 0, tiled=True).reshape(1, NA, V)  23.3 us
    ppermute x2, starting transfers between devices, ahead(): lax.ppermute(x, ('blk_far', 'blk_near'), [(i, (i - shift) % NZ) for i in...  7.09 us
    all_to_all x1, starting transfers between devices, on_device(): lax.all_to_all(jnp.broadcast_to(own, (NP, NA, V)), 'blk_y', 0, 0, tiled=T...  5.91 us
    pallas_call x2, Pallas kernels, pair_terms(): pl.pallas_call(functools.partial(pair_kernel, parity, before is not None)...  5.08 us
    ppermute x2, waiting for transfers between devices, ahead(): lax.ppermute(x, ('blk_far', 'blk_near'), [(i, (i - shift) % NZ) for i in...  2.64 us
  transfers between devices with their start and end apart: 3, of which 2 were waited for; matrix products, arithmetic and copies ran while one was open for 0% of the time, Pallas kernels for 2%

profile of v4, /device:TPU:1, one launch (start us, length us, event | category | flops | bytes accessed | tf_op | source)
XLA Modules:
  0.0 106.0 jit_solution(14826385569712617819)
XLA Ops:
  0.0 23.3 %all_to_all.15 = bf16[16,16,128]{2,1,0:T(8,128)(2,1)S(1)} all-to-all(bf16[16,16,128]{2,1,0:T(8,128)(2,1)} %bitcast.21), channel_id=1, replica_groups=mesh['aux_x'=4,'aux_y'=2,'aux_core'=2,'blk_y'=4,'blk_far'=8,'blk_near'=2..., dimensions={0} | all-to-all | bytes 131072 | tf_op jit(solution)/shard_map/all_to_all | solution.py:100
  23.3 26.0 %all_gather.3.refs_0_ = bf16[8,256,128]{2,1,0:T(8,128)(2,1)S(1)} all-gather(bf16[1,256,128]{2,1,0:T(8,128)(2,1)S(1)} %bitcast.19), channel_id=1, replica_groups=mesh['aux_x'=4,'aux_y'=2,'aux_core'=2,'blk_y'=4,'blk_far'=8,'blk_near'=2..., dimensions={0}, use_global_device_ids=true | all-gather | bytes 589824 | tf_op jit(solution)/shard_map/all_gather | solution.py:101
  49.3 0.7 broadcast_in_dim.11
  50.1 5.9 %all-to-all-start.1 = ((bf16[4,256,128]{2,1,0:T(8,128)(2,1)}), bf16[4,256,128]{2,1,0:T(8,128)(2,1)S(1)}, u32[]{:S(2)}, u32[]{:S(2)}) async-start(bf16[4,256,128]{2,1,0:T(8,128)(2,1)} %broadcast_in_dim.11), calls=%async_computation.1 | async-start | bytes 524288 | tf_op jit(solution)/shard_map/all_to_all | solution.py:103
  56.0 0.0 copy-start
  56.0 0.0 copy-start.3
  56.0 5.2 %collective-permute-start = (bf16[4,256,128]{2,1,0:T(8,128)(2,1)S(1)}, bf16[4,256,128]{2,1,0:T(8,128)(2,1)S(1)}, u32[]{:S(2)}, u32[]{:S(2)}) collective-permute-start(bf16[4,256,128]{2,1,0:T(8,128)(2,1)S(1)} %get-tuple-element.10), channel_id=1, source_target_pairs={{0,15},{1,0},{2,1},{3,2},{4,3},{5,4},{6,5},{7,6},{8,7},{9,8},{10,9... | collective-permute-start | bytes 786440 | tf_op jit(solution)/shard_map/ppermute | solution.py:96
  61.2 1.9 %collective-permute-start.1 = (bf16[4,256,128]{2,1,0:T(8,128)(2,1)S(1)}, bf16[4,256,128]{2,1,0:T(8,128)(2,1)S(1)}, u32[]{:S(2)}, u32[]{:S(2)}) collective-permute-start(bf16[4,256,128]{2,1,0:T(8,128)(2,1)S(1)} %get-tuple-element.9), channel_id=1, source_target_pairs={{0,1},{1,2},{2,3},{3,4},{4,5},{5,6},{6,7},{7,8},{8,9},{9,10},{10,1... | collective-permute-start | bytes 786440 | tf_op jit(solution)/shard_map/ppermute | solution.py:96
  63.1 0.8 all-to-all-done.1.p_ref
  63.9 0.0 copy-start.1
  63.9 0.0 copy-start.2
  64.0 0.0 copy-done
  64.0 0.0 copy-done.3
  64.0 0.7 copy-done.1
  64.6 0.0 copy-done.2
  64.6 2.5 %shard_map.55.refs_2_ = f32[256,512]{1,0:T(8,128)S(1)} custom-call(s32[2,64]{1,0:T(2,128)S(1)} %bitcast.14, s32[64,64]{1,0:T(8,128)S(1)} %bitcast.12, f32[1,64]{1,0:T(1,128)S(1)} %bitcast.16, f32[1,128]{1,0:T(1,128)S(1)} %copy-done.3, bf16[4,256,128]{2,1,0:T(8,128)(2,1)S(1)} %all-to-all-done.1.p_ref, bf16[8,256,128]{2,1,0:T(8,128)(2,1)S(1)} %all_gather.3.refs_0_), custom_call_target="tpu_custom_call" | custom-call | flops 1000000000 | bytes 2000000 | tf_op jit(solution)/shard_map/pallas_call | solution.py:79
  67.2 0.0 collective-permute-done.refs_0_
  67.2 2.6 %collective-permute-done.1.refs_1_ = bf16[4,256,128]{2,1,0:T(8,128)(2,1)S(1)} collective-permute-done((bf16[4,256,128]{2,1,0:T(8,128)(2,1)S(1)}, bf16[4,256,128]{2,1,0:T(8,128)(2,1)S(1)}, u32[]{:S(2)}, u32[]{:S(2)}) %collective-permute-start.1) | collective-permute-done | bytes 262176 | tf_op jit(solution)/shard_map/ppermute | solution.py:96
  69.8 2.5 %shard_map.56 = f32[4,16,16,128]{3,2,1,0:T(8,128)S(1)} custom-call(s32[2,64]{1,0:T(2,128)S(1)} %bitcast.15, s32[64,64]{1,0:T(8,128)S(1)} %bitcast.13, f32[1,64]{1,0:T(1,128)S(1)} %bitcast.17, f32[1,128]{1,0:T(1,128)S(1)} %copy-done.3, bf16[4,256,128]{2,1,0:T(8,128)(2,1)S(1)} %all-to-all-done.1.p_ref, bf16[4,256,128]{2,1,0:T(8,128)(2,1)S(1)} %collective-permute-done.refs_0_, ...), custom_call_target="tpu_custom_call" | custom-call | flops 1000000000 | bytes 2000000 | tf_op jit(solution)/shard_map/pallas_call | solution.py:79
  72.4 33.0 %all_to_all.16 = f32[64,16,128]{2,1,0:T(8,128)S(1)} all-to-all(f32[64,16,128]{2,1,0:T(8,128)S(1)} %bitcast.11), channel_id=1, replica_groups=mesh['aux_x'=4,'aux_y'=2,'aux_core'=2,'blk_y'=4,'blk_far'=8,'blk_near'=2..., dimensions={0} | all-to-all | bytes 1048576 | tf_op jit(solution)/shard_map/all_to_all | solution.py:108
  105.3 0.7 reduce_sum.9
  (1 shorter events, 0.0 us)
Async XLA Ops:
  50.1 13.9 %all-to-all-start.1 = ((bf16[4,256,128]{2,1,0:T(8,128)(2,1)}), bf16[4,256,128]{2,1,0:T(8,128)(2,1)S(1)}, u32[]{:S(2)}, u32[]{:S(2)}) async-start(bf16[4,256,128]{2,1,0:T(8,128)(2,1)} %broadcast_in_dim.11), calls=%async_computation.1 | async-start | bytes 524288 | tf_op jit(solution)/shard_map/all_to_all | solution.py:103
  56.0 8.0 %copy-start = (s32[1,64,64]{2,1,0:T(8,128)S(1)}, s32[1,64,64]{2,1,0:T(8,128)}, u32[]{:S(2)}) copy-start(s32[1,64,64]{2,1,0:T(8,128)} %param.7) | copy-start | bytes 49156
  56.0 8.0 %copy-start.3 = (f32[1,128]{1,0:T(1,128)S(1)}, f32[1,128]{1,0:T(1,128)}, u32[]{:S(2)}) copy-start(f32[1,128]{1,0:T(1,128)} %virt.3) | copy-start | bytes 1540
  56.0 11.2 %collective-permute-start = (bf16[4,256,128]{2,1,0:T(8,128)(2,1)S(1)}, bf16[4,256,128]{2,1,0:T(8,128)(2,1)S(1)}, u32[]{:S(2)}, u32[]{:S(2)}) collective-permute-start(bf16[4,256,128]{2,1,0:T(8,128)(2,1)S(1)} %get-tuple-element.10), channel_id=1, source_target_pairs={{0,15},{1,0},{2,1},{3,2},{4,3},{5,4},{6,5},{7,6},{8,7},{9,8},{10,9... | collective-permute-start | bytes 786440 | tf_op jit(solution)/shard_map/ppermute | solution.py:96
  61.2 8.6 %collective-permute-start.1 = (bf16[4,256,128]{2,1,0:T(8,128)(2,1)S(1)}, bf16[4,256,128]{2,1,0:T(8,128)(2,1)S(1)}, u32[]{:S(2)}, u32[]{:S(2)}) collective-permute-start(bf16[4,256,128]{2,1,0:T(8,128)(2,1)S(1)} %get-tuple-element.9), channel_id=1, source_target_pairs={{0,1},{1,2},{2,3},{3,4},{4,5},{5,6},{6,7},{7,8},{8,9},{9,10},{10,1... | collective-permute-start | bytes 786440 | tf_op jit(solution)/shard_map/ppermute | solution.py:96
  63.9 0.7 copy-start.1
  63.9 0.7 copy-start.2

commit v5 on v4

v5 whole, which is shorter than its diff:
```python
import jax
import jax.numpy as jnp
from jax import lax
from jax.experimental import pallas as pl
from jax.experimental.pallas import tpu as pltpu
from jax.sharding import Mesh, PartitionSpec as P

AUX = ("aux_x", "aux_y", "aux_core")
NP = 4
NZ = 16
SCALE = 2.0**14
V = 128
AB = 128
NA = 256


def pair_kernel(sig, keep, occ, virt, p_ref, q_ref, out, pcat, pcat_t, vb, acc):
    h = lax.axis_index("blk_y")
    w = lax.axis_index("blk_z")
    rows = lax.broadcasted_iota(jnp.int32, (NA, V), 0)
    zero = jnp.zeros((NA, V), jnp.bfloat16)

    def live(orbital):
        return jnp.where(rows < AB, sig[0, orbital], sig[1, orbital]) > 0

    p_index = [s * NZ + w for s in range(NP)]
    for s in range(NP):
        block = jnp.where(live(p_index[s]), p_ref[s], zero) * (1 / SCALE)
        pcat[:, s * V : (s + 1) * V] = block * 2
        pcat_t[s * V : (s + 1) * V, :] = block.T
    q_index = [h * NZ + k for k in range(NZ)]
    va = virt[...]
    vb[...] = jnp.broadcast_to(va, (V, V)).T
    for c in range(0, NZ, 2):
        block = jnp.concatenate([jnp.where(live(q_index[c + t]), q_ref[c + t], zero) for t in range(2)], axis=1)
        twice = jnp.dot(block.T, pcat[...], preferred_element_type=jnp.float32)
        swapped = jnp.dot(pcat_t[...], block, preferred_element_type=jnp.float32)
        columns = []
        for s in range(NP):
            tiles = []
            for t in range(2):
                p, q = p_index[s], q_index[c + t]
                kept = keep[lax.min(p, q), lax.max(p, q)].astype(jnp.float32)
                total = occ[0, p] + occ[0, q]
                top = twice[t * V : (t + 1) * V, s * V : (s + 1) * V]
                top = top - swapped[s * V : (s + 1) * V, t * V : (t + 1) * V]
                tiles.append((kept * top / ((total - va) - vb[...])).astype(jnp.bfloat16))
            columns.append(jnp.concatenate(tiles, axis=0))
        tilde = jnp.concatenate(columns, axis=1)
        gamma = jnp.dot(block, tilde, preferred_element_type=jnp.float32)
        if c == 0:
            acc[...] = gamma
        else:
            acc[...] += gamma
    for s in range(NP):
        gamma = jnp.where(live(p_index[s]), acc[:, s * V : (s + 1) * V], 0.0) * (1 / SCALE)
        out[s] = gamma.reshape(16, 16, V)


def pair_terms(scalars, p_blocks, q_blocks):
    smem = pl.BlockSpec(memory_space=pltpu.SMEM)
    vmem = pl.BlockSpec(memory_space=pltpu.VMEM)
    return pl.pallas_call(
        pair_kernel,
        out_shape=jax.ShapeDtypeStruct((NP, 16, 16, V), jnp.float32),
        in_specs=[smem] * 3 + [vmem] * 3,
        out_specs=vmem,
        scratch_shapes=[
            pltpu.VMEM((NA, NP * V), jnp.bfloat16),
            pltpu.VMEM((NP * V, NA), jnp.bfloat16),
            pltpu.VMEM((V, V), jnp.float32),
            pltpu.VMEM((NA, NP * V), jnp.float32),
        ],
        compiler_params=pltpu.CompilerParams(vmem_limit_bytes=24 * 2**20),
        cost_estimate=pl.CostEstimate(flops=2 * 10**9, bytes_accessed=2 * 10**6, transcendentals=10**6),
    )(*scalars, p_blocks, q_blocks)


def on_device(b_tensor, significance, pair_keep, occ_energy, virt_energy):
    own = lax.all_to_all(b_tensor[0], AUX, 0, 0, tiled=True).reshape(1, NA, V)
    sent = (own.astype(jnp.float32) * SCALE).astype(jnp.float16)
    line = lax.all_gather(sent, "blk_z", axis=0, tiled=True)
    own, line = lax.optimization_barrier((own, line))
    p_blocks = lax.all_to_all(jnp.broadcast_to(own, (NP, NA, V)), "blk_y", 0, 0, tiled=True)
    scalars = (significance[:, 0, :].T, pair_keep[0], occ_energy.T, virt_energy)
    part = pair_terms(scalars, p_blocks, line.astype(jnp.bfloat16))
    back = lax.all_to_all(part.reshape(64, 16, V), ("blk_y",) + AUX, 0, 0, tiled=True)
    return back.reshape(NP, 16, 16, V).sum(axis=0)[None]


def solution(mesh):
    blk = ("blk_y", "blk_z")
    fine = Mesh(mesh.devices.reshape(4, 2, 2, NP, NZ), AUX + blk)
    return jax.shard_map(
        on_device,
        mesh=fine,
        in_specs=(
            P(blk, None, AUX, None),
            P(None, AUX, None),
            P(AUX, None, None),
            P(None, AUX),
            P(AUX, None),
        ),
        out_specs=P(blk, None, AUX, None),
        check_vma=False,
    )
```

time: 106 us -> 104 us (0.981)
  starting transfers between devices: 13 us -> 5.91 us
  waiting for transfers between devices: 3.46 us -> 7.72 us
  blocking collectives: 82.3 us -> 84.2 us
  Pallas kernels: 5.08 us -> 3.64 us
    ppermute x2 -> x0, starting transfers between devices: 7.09 us -> none  [ahead(): lax.ppermute(x, ('blk_far', 'blk_near'), [(i, (i - shift) % NZ) for i in...]
    all_to_all x1, waiting for transfers between devices: 0.82 us -> 7.72 us  [on_device(): lax.all_to_all(jnp.broadcast_to(own, (NP, NA, V)), 'blk_y', 0, 0, tiled=T...]
    all_gather x1, blocking collectives: 26 us -> 30.8 us  [on_device(): line = lax.all_gather(sent, 'blk_z', axis=0, tiled=True)]
    all_to_all x1, blocking collectives: 33 us -> 30.1 us  [on_device(): lax.all_to_all(part.reshape(64, 16, V), ('blk_y',) + AUX, 0, 0, tiled=True)]
    ppermute x2 -> x0, waiting for transfers between devices: 2.64 us -> none  [ahead(): lax.ppermute(x, ('blk_far', 'blk_near'), [(i, (i - shift) % NZ) for i in...]
    pallas_call x2 -> x1, Pallas kernels: 5.08 us -> 3.64 us  [pair_terms(): pl.pallas_call(pair_kernel, out_shape=jax.ShapeDtypeStruct((NP, 16, 16, V...]
  transfers between devices with their start and end apart: 3 -> 1, of which waited for: 2 -> 1; matrix products, arithmetic and copies ran while one was open for 0% -> 0% of each run, Pallas kernels for 2% -> 0%
where the time goes in v5:
time: 104 us
  blocking collectives  84.2 us (81%)
  waiting for transfers between devices  7.72 us (7%)
  starting transfers between devices  5.91 us (6%)
  Pallas kernels  3.64 us (4%)
  local copies, waits for them, and re-layouts  1.4 us (1%)
    all_gather x1, blocking collectives, on_device(): line = lax.all_gather(sent, 'blk_z', axis=0, tiled=True)  30.8 us
    all_to_all x1, blocking collectives, on_device(): lax.all_to_all(part.reshape(64, 16, V), ('blk_y',) + AUX, 0, 0, tiled=True)  30.1 us
    all_to_all x1, blocking collectives, on_device(): own = lax.all_to_all(b_tensor[0], AUX, 0, 0, tiled=True).reshape(1, NA, V)  23.3 us
    all_to_all x1, waiting for transfers between devices, on_device(): lax.all_to_all(jnp.broadcast_to(own, (NP, NA, V)), 'blk_y', 0, 0, tiled=T...  7.72 us
    all_to_all x1, starting transfers between devices, on_device(): lax.all_to_all(jnp.broadcast_to(own, (NP, NA, V)), 'blk_y', 0, 0, tiled=T...  5.91 us
    pallas_call x1, Pallas kernels, pair_terms(): pl.pallas_call(pair_kernel, out_shape=jax.ShapeDtypeStruct((NP, 16, 16, V...  3.64 us
  transfers between devices with their start and end apart: 1, of which 1 were waited for; matrix products, arithmetic and copies ran while one was open for 0% of the time, Pallas kernels for 0%

profile of v5, /device:TPU:1, one launch (start us, length us, event | category | flops | bytes accessed | tf_op | source)
XLA Modules:
  0.0 103.8 jit_solution(5693539828422091279)
XLA Ops:
  0.0 23.3 %all_to_all.15 = bf16[16,16,128]{2,1,0:T(8,128)(2,1)S(1)} all-to-all(bf16[16,16,128]{2,1,0:T(8,128)(2,1)} %bitcast.20), channel_id=1, replica_groups=mesh['aux_x'=4,'aux_y'=2,'aux_core'=2,'blk_y'=4,'blk_z'=16] {'aux_x','au..., dimensions={0} | all-to-all | bytes 131072 | tf_op jit(solution)/shard_map/all_to_all | solution.py:80
  23.3 30.8 %all-gather.1 = f16[16,256,128]{2,1,0:T(8,128)(2,1)S(1)} all-gather(f16[1,256,128]{2,1,0:T(8,128)(2,1)S(1)} %multiply_convert_fusion), channel_id=1, replica_groups=mesh['aux_x'=4,'aux_y'=2,'aux_core'=2,'blk_y'=4,'blk_z'=16] {'blk_z'}, dimensions={0}, use_global_device_ids=true | all-gather | bytes 1114112 | tf_op jit(solution)/shard_map/all_gather | solution.py:82
  54.1 0.7 broadcast_in_dim.11
  54.8 5.9 %all-to-all-start.1 = ((bf16[4,256,128]{2,1,0:T(8,128)(2,1)}), bf16[4,256,128]{2,1,0:T(8,128)(2,1)S(1)}, u32[]{:S(2)}, u32[]{:S(2)}) async-start(bf16[4,256,128]{2,1,0:T(8,128)(2,1)} %broadcast_in_dim.11), calls=%async_computation.1 | async-start | bytes 524288 | tf_op jit(solution)/shard_map/all_to_all | solution.py:84
  60.8 0.0 copy-start
  60.8 0.0 copy-start.3
  60.8 0.2 convert_element_type.27.q_ref
  61.0 7.7 %all-to-all-done.1.p_ref = bf16[4,256,128]{2,1,0:T(8,128)(2,1)S(1)} async-done(((bf16[4,256,128]{2,1,0:T(8,128)(2,1)}), bf16[4,256,128]{2,1,0:T(8,128)(2,1)S(1)}, u32[]{:S(2)}, u32[]{:S(2)}) %all-to-all-start.1) | async-done | bytes 262176 | tf_op jit(solution)/shard_map/all_to_all | solution.py:84
  68.7 0.0 copy-start.1
  68.7 0.0 copy-start.2
  68.7 0.0 copy-done
  68.7 0.0 copy-done.3
  68.7 0.7 copy-done.1
  69.4 0.0 copy-done.2
  69.4 3.6 %shard_map.55 = f32[4,16,16,128]{3,2,1,0:T(8,128)S(1)} custom-call(s32[2,64]{1,0:T(2,128)S(1)} %bitcast.15, s32[64,64]{1,0:T(8,128)S(1)} %bitcast.14, f32[1,64]{1,0:T(1,128)S(1)} %bitcast.16, f32[1,128]{1,0:T(1,128)S(1)} %copy-done.3, bf16[4,256,128]{2,1,0:T(8,128)(2,1)S(1)} %all-to-all-done.1.p_ref, bf16[16,256,128]{2,1,0:T(8,128)(2,1)S(1)} %convert_element_type.27.q_ref), custom_call_target="tpu_custom_call" | custom-call | flops 2000000000 | bytes 2000000 | tf_op jit(solution)/shard_map/pallas_call | solution.py:63
  73.0 30.1 %all_to_all.16 = f32[64,16,128]{2,1,0:T(8,128)S(1)} all-to-all(f32[64,16,128]{2,1,0:T(8,128)S(1)} %bitcast.13), channel_id=1, replica_groups=mesh['aux_x'=4,'aux_y'=2,'aux_core'=2,'blk_y'=4,'blk_z'=16] {'blk_y','au..., dimensions={0} | all-to-all | bytes 1048576 | tf_op jit(solution)/shard_map/all_to_all | solution.py:87
  103.1 0.7 reduce_sum.9
  (1 shorter events, 0.0 us)
Async XLA Ops:
  54.8 13.8 %all-to-all-start.1 = ((bf16[4,256,128]{2,1,0:T(8,128)(2,1)}), bf16[4,256,128]{2,1,0:T(8,128)(2,1)S(1)}, u32[]{:S(2)}, u32[]{:S(2)}) async-start(bf16[4,256,128]{2,1,0:T(8,128)(2,1)} %broadcast_in_dim.11), calls=%async_computation.1 | async-start | bytes 524288 | tf_op jit(solution)/shard_map/all_to_all | solution.py:84
  60.8 7.9 %copy-start = (s32[1,64,64]{2,1,0:T(8,128)S(1)}, s32[1,64,64]{2,1,0:T(8,128)}, u32[]{:S(2)}) copy-start(s32[1,64,64]{2,1,0:T(8,128)} %param.7) | copy-start | bytes 49156
  60.8 7.9 %copy-start.3 = (f32[1,128]{1,0:T(1,128)S(1)}, f32[1,128]{1,0:T(1,128)}, u32[]{:S(2)}) copy-start(f32[1,128]{1,0:T(1,128)} %virt.1) | copy-start | bytes 1540
  68.7 0.7 copy-start.1
  68.7 0.7 copy-start.2

commit v6 on v5

--- a/solution.py
+++ b/solution.py
@@ -78,10 +78,9 @@
 
 def on_device(b_tensor, significance, pair_keep, occ_energy, virt_energy):
     own = lax.all_to_all(b_tensor[0], AUX, 0, 0, tiled=True).reshape(1, NA, V)
+    p_blocks = lax.all_to_all(jnp.broadcast_to(own, (NP, NA, V)), "blk_y", 0, 0, tiled=True)
     sent = (own.astype(jnp.float32) * SCALE).astype(jnp.float16)
     line = lax.all_gather(sent, "blk_z", axis=0, tiled=True)
-    own, line = lax.optimization_barrier((own, line))
-    p_blocks = lax.all_to_all(jnp.broadcast_to(own, (NP, NA, V)), "blk_y", 0, 0, tiled=True)
     scalars = (significance[:, 0, :].T, pair_keep[0], occ_energy.T, virt_energy)
     part = pair_terms(scalars, p_blocks, line.astype(jnp.bfloat16))
     back = lax.all_to_all(part.reshape(64, 16, V), ("blk_y",) + AUX, 0, 0, tiled=True)

time: 104 us -> 99.3 us (0.955)
  waiting for transfers between devices: 7.72 us -> 0.01 us
  blocking collectives: 84.2 us -> 89.5 us
  starting transfers between devices: 5.91 us -> 3.4 us
    all_to_all x1, waiting for transfers between devices: 7.72 us -> 0.01 us  [on_device(): lax.all_to_all(jnp.broadcast_to(own, (NP, NA, V)), 'blk_y', 0, 0, tiled=T...]
    all_to_all x1, blocking collectives: 30.1 us -> 32.8 us  [on_device(): lax.all_to_all(part.reshape(64, 16, V), ('blk_y',) + AUX, 0, 0, tiled=True)]
    all_gather x1, blocking collectives: 30.8 us -> 33.4 us  [on_device(): line = lax.all_gather(sent, 'blk_z', axis=0, tiled=True)]
    all_to_all x1, starting transfers between devices: 5.91 us -> 3.4 us  [on_device(): lax.all_to_all(jnp.broadcast_to(own, (NP, NA, V)), 'blk_y', 0, 0, tiled=T...]
  transfers between devices with their start and end apart: 1 -> 1, of which waited for: 1 -> 0; matrix products, arithmetic and copies ran while one was open for 0% -> 0% of each run, Pallas kernels for 0% -> 0%
where the time goes in v6:
time: 99.3 us; the launch traced here: 98.9 us
  blocking collectives  89.5 us (90%)
  Pallas kernels  3.64 us (4%)
  starting transfers between devices  3.4 us (3%)
  local copies, waits for them, and re-layouts  1.4 us (1%)
    all_gather x1, blocking collectives, on_device(): line = lax.all_gather(sent, 'blk_z', axis=0, tiled=True)  33.4 us
    all_to_all x1, blocking collectives, on_device(): lax.all_to_all(part.reshape(64, 16, V), ('blk_y',) + AUX, 0, 0, tiled=True)  32.8 us
    all_to_all x1, blocking collectives, on_device(): own = lax.all_to_all(b_tensor[0], AUX, 0, 0, tiled=True).reshape(1, NA, V)  23.3 us
    pallas_call x1, Pallas kernels, pair_terms(): pl.pallas_call(pair_kernel, out_shape=jax.ShapeDtypeStruct((NP, 16, 16, V...  3.64 us
    all_to_all x1, starting transfers between devices, on_device(): lax.all_to_all(jnp.broadcast_to(own, (NP, NA, V)), 'blk_y', 0, 0, tiled=T...  3.4 us
  transfers between devices with their start and end apart: 1, of which 0 were waited for; matrix products, arithmetic and copies ran while one was open for 0% of the time, Pallas kernels for 0%

profile of v6, /device:TPU:1, one launch (start us, length us, event | category | flops | bytes accessed | tf_op | source)
XLA Modules:
  0.0 98.9 jit_solution(16749989848809804778)
XLA Ops:
  0.0 23.3 %all_to_all.15 = bf16[16,16,128]{2,1,0:T(8,128)(2,1)S(1)} all-to-all(bf16[16,16,128]{2,1,0:T(8,128)(2,1)} %bitcast.18), channel_id=1, replica_groups=mesh['aux_x'=4,'aux_y'=2,'aux_core'=2,'blk_y'=4,'blk_z'=16] {'aux_x','au..., dimensions={0} | all-to-all | bytes 131072 | tf_op jit(solution)/shard_map/all_to_all | solution.py:80
  23.3 0.7 broadcast_in_dim.11
  24.0 3.4 %all-to-all-start.1 = ((bf16[4,256,128]{2,1,0:T(8,128)(2,1)}), bf16[4,256,128]{2,1,0:T(8,128)(2,1)S(1)}, u32[]{:S(2)}, u32[]{:S(2)}) async-start(bf16[4,256,128]{2,1,0:T(8,128)(2,1)} %broadcast_in_dim.11), calls=%async_computation.1 | async-start | bytes 524288 | tf_op jit(solution)/shard_map/all_to_all | solution.py:81
  27.5 33.4 %all-gather.1 = f16[16,256,128]{2,1,0:T(8,128)(2,1)S(1)} all-gather(f16[1,256,128]{2,1,0:T(8,128)(2,1)S(1)} %bitcast.17), channel_id=1, replica_groups=mesh['aux_x'=4,'aux_y'=2,'aux_core'=2,'blk_y'=4,'blk_z'=16] {'blk_z'}, dimensions={0}, use_global_device_ids=true | all-gather | bytes 1114112 | tf_op jit(solution)/shard_map/all_gather | solution.py:83
  60.8 0.0 copy-start
  60.8 0.0 copy-start.3
  60.8 0.2 convert_element_type.32.q_ref
  61.1 0.0 all-to-all-done.1.p_ref
  61.1 0.0 copy-start.1
  61.1 0.0 copy-start.2
  61.1 0.5 copy-done
  61.6 0.0 copy-done.3
  61.6 0.1 copy-done.1
  61.7 0.0 copy-done.2
  61.8 3.6 %shard_map.55 = f32[4,16,16,128]{3,2,1,0:T(8,128)S(1)} custom-call(s32[2,64]{1,0:T(2,128)S(1)} %bitcast.13, s32[64,64]{1,0:T(8,128)S(1)} %bitcast.12, f32[1,64]{1,0:T(1,128)S(1)} %bitcast.14, f32[1,128]{1,0:T(1,128)S(1)} %copy-done.3, bf16[4,256,128]{2,1,0:T(8,128)(2,1)S(1)} %all-to-all-done.1.p_ref, bf16[16,256,128]{2,1,0:T(8,128)(2,1)S(1)} %convert_element_type.32.q_ref), custom_call_target="tpu_custom_call" | custom-call | flops 2000000000 | bytes 2000000 | tf_op jit(solution)/shard_map/pallas_call | solution.py:63
  65.4 32.8 %all_to_all.16 = f32[64,16,128]{2,1,0:T(8,128)S(1)} all-to-all(f32[64,16,128]{2,1,0:T(8,128)S(1)} %bitcast.11), channel_id=1, replica_groups=mesh['aux_x'=4,'aux_y'=2,'aux_core'=2,'blk_y'=4,'blk_z'=16] {'blk_y','au..., dimensions={0} | all-to-all | bytes 1048576 | tf_op jit(solution)/shard_map/all_to_all | solution.py:86
  98.2 0.7 reduce_sum.9
  (1 shorter events, 0.0 us)
Async XLA Ops:
  24.0 37.0 %all-to-all-start.1 = ((bf16[4,256,128]{2,1,0:T(8,128)(2,1)}), bf16[4,256,128]{2,1,0:T(8,128)(2,1)S(1)}, u32[]{:S(2)}, u32[]{:S(2)}) async-start(bf16[4,256,128]{2,1,0:T(8,128)(2,1)} %broadcast_in_dim.11), calls=%async_computation.1 | async-start | bytes 524288 | tf_op jit(solution)/shard_map/all_to_all | solution.py:81
  60.8 0.8 copy-start
  60.8 0.8 copy-start.3
  61.1 0.7 copy-start.1
  61.1 0.7 copy-start.2

commit v7 on v6

--- a/solution.py
+++ b/solution.py
@@ -14,7 +14,17 @@
 NA = 256
 
 
-def pair_kernel(sig, keep, occ, virt, p_ref, q_ref, out, pcat, pcat_t, vb, acc):
+def pair_kernel(sig_hbm, keep_hbm, occ_hbm, virt, p_ref, q_ref, out, pcat, pcat_t, vb, sig, keep, occ, done):
+    copies = [
+        pltpu.make_async_copy(src, dst, done.at[i])
+        for i, (src, dst) in enumerate(((sig_hbm, sig), (keep_hbm, keep), (occ_hbm, occ)))
+    ]
+    for copy in copies:
+        copy.start()
+    va = virt[...]
+    vb[...] = jnp.broadcast_to(va, (V, V)).T
+    for copy in copies:
+        copy.wait()
     h = lax.axis_index("blk_y")
     w = lax.axis_index("blk_z")
     rows = lax.broadcasted_iota(jnp.int32, (NA, V), 0)
@@ -29,8 +39,7 @@
         pcat[:, s * V : (s + 1) * V] = block * 2
         pcat_t[s * V : (s + 1) * V, :] = block.T
     q_index = [h * NZ + k for k in range(NZ)]
-    va = virt[...]
-    vb[...] = jnp.broadcast_to(va, (V, V)).T
+    qs, ts = [], []
     for c in range(0, NZ, 2):
         block = jnp.concatenate([jnp.where(live(q_index[c + t]), q_ref[c + t], zero) for t in range(2)], axis=1)
         twice = jnp.dot(block.T, pcat[...], preferred_element_type=jnp.float32)
@@ -47,29 +56,30 @@
                 tiles.append((kept * top / ((total - va) - vb[...])).astype(jnp.bfloat16))
             columns.append(jnp.concatenate(tiles, axis=0))
         tilde = jnp.concatenate(columns, axis=1)
-        gamma = jnp.dot(block, tilde, preferred_element_type=jnp.float32)
-        if c == 0:
-            acc[...] = gamma
-        else:
-            acc[...] += gamma
+        qs.append(block)
+        ts.append(tilde)
+    gammas = jnp.dot(jnp.concatenate(qs, axis=1), jnp.concatenate(ts, axis=0), preferred_element_type=jnp.float32)
     for s in range(NP):
-        gamma = jnp.where(live(p_index[s]), acc[:, s * V : (s + 1) * V], 0.0) * (1 / SCALE)
+        gamma = jnp.where(live(p_index[s]), gammas[:, s * V : (s + 1) * V], 0.0) * (1 / SCALE)
         out[s] = gamma.reshape(16, 16, V)
 
 
 def pair_terms(scalars, p_blocks, q_blocks):
-    smem = pl.BlockSpec(memory_space=pltpu.SMEM)
+    hbm = pl.BlockSpec(memory_space=pltpu.HBM)
     vmem = pl.BlockSpec(memory_space=pltpu.VMEM)
     return pl.pallas_call(
         pair_kernel,
         out_shape=jax.ShapeDtypeStruct((NP, 16, 16, V), jnp.float32),
-        in_specs=[smem] * 3 + [vmem] * 3,
+        in_specs=[hbm] * 3 + [vmem] * 3,
         out_specs=vmem,
         scratch_shapes=[
             pltpu.VMEM((NA, NP * V), jnp.bfloat16),
             pltpu.VMEM((NP * V, NA), jnp.bfloat16),
             pltpu.VMEM((V, V), jnp.float32),
-            pltpu.VMEM((NA, NP * V), jnp.float32),
+            pltpu.SMEM((2, NP * NZ), jnp.int32),
+            pltpu.SMEM((NP * NZ, NP * NZ), jnp.int32),
+            pltpu.SMEM((1, NP * NZ), jnp.float32),
+            pltpu.SemaphoreType.DMA((3,)),
         ],
         compiler_params=pltpu.CompilerParams(vmem_limit_bytes=24 * 2**20),
         cost_estimate=pl.CostEstimate(flops=2 * 10**9, bytes_accessed=2 * 10**6, transcendentals=10**6),

time: 99.3 us -> 98.7 us (level)
  no operation moved by 1% of the time
where the time goes in v7:
time: 98.7 us; the launch traced here: 98.3 us
  blocking collectives  89.5 us (91%)
  starting transfers between devices  3.4 us (3%)
  Pallas kernels  3.05 us (3%)
  local copies, waits for them, and re-layouts  1.4 us (1%)
    all_gather x1, blocking collectives, on_device(): line = lax.all_gather(sent, 'blk_z', axis=0, tiled=True)  33.4 us
    all_to_all x1, blocking collectives, on_device(): lax.all_to_all(part.reshape(64, 16, V), ('blk_y',) + AUX, 0, 0, tiled=True)  32.8 us
    all_to_all x1, blocking collectives, on_device(): own = lax.all_to_all(b_tensor[0], AUX, 0, 0, tiled=True).reshape(1, NA, V)  23.3 us
    all_to_all x1, starting transfers between devices, on_device(): lax.all_to_all(jnp.broadcast_to(own, (NP, NA, V)), 'blk_y', 0, 0, tiled=T...  3.4 us
    pallas_call x1, Pallas kernels, pair_terms(): pl.pallas_call(pair_kernel, out_shape=jax.ShapeDtypeStruct((NP, 16, 16, V...  3.05 us
  transfers between devices with their start and end apart: 1, of which 0 were waited for; matrix products, arithmetic and copies ran while one was open for 0% of the time, Pallas kernels for 0%

profile of v7, /device:TPU:1, one launch (start us, length us, event | category | flops | bytes accessed | tf_op | source)
XLA Modules:
  0.0 98.3 jit_solution(10329856020350992199)
XLA Ops:
  0.0 23.3 %all_to_all.15 = bf16[16,16,128]{2,1,0:T(8,128)(2,1)S(1)} all-to-all(bf16[16,16,128]{2,1,0:T(8,128)(2,1)} %bitcast.18), channel_id=1, replica_groups=mesh['aux_x'=4,'aux_y'=2,'aux_core'=2,'blk_y'=4,'blk_z'=16] {'aux_x','au..., dimensions={0} | all-to-all | bytes 131072 | tf_op jit(solution)/shard_map/all_to_all | solution.py:90
  23.3 0.7 broadcast_in_dim.11
  24.0 3.4 %all-to-all-start.1 = ((bf16[4,256,128]{2,1,0:T(8,128)(2,1)}), bf16[4,256,128]{2,1,0:T(8,128)(2,1)S(1)}, u32[]{:S(2)}, u32[]{:S(2)}) async-start(bf16[4,256,128]{2,1,0:T(8,128)(2,1)} %broadcast_in_dim.11), calls=%async_computation.1 | async-start | bytes 524288 | tf_op jit(solution)/shard_map/all_to_all | solution.py:91
  27.5 33.4 %all-gather.1 = f16[16,256,128]{2,1,0:T(8,128)(2,1)S(1)} all-gather(f16[1,256,128]{2,1,0:T(8,128)(2,1)S(1)} %bitcast.17), channel_id=1, replica_groups=mesh['aux_x'=4,'aux_y'=2,'aux_core'=2,'blk_y'=4,'blk_z'=16] {'blk_z'}, dimensions={0}, use_global_device_ids=true | all-gather | bytes 1114112 | tf_op jit(solution)/shard_map/all_gather | solution.py:93
  60.8 0.0 copy-start
  60.8 0.0 copy-start.3
  60.8 0.2 convert_element_type.32.q_ref
  61.1 0.0 all-to-all-done.1.p_ref
  61.1 0.0 copy-start.1
  61.1 0.0 copy-start.2
  61.1 0.5 copy-done
  61.6 0.0 copy-done.3
  61.6 0.1 copy-done.1
  61.7 0.0 copy-done.2
  61.8 3.1 %shard_map.55 = f32[4,16,16,128]{3,2,1,0:T(8,128)S(1)} custom-call(s32[2,64]{1,0:T(2,128)S(1)} %bitcast.13, s32[64,64]{1,0:T(8,128)S(1)} %bitcast.12, f32[1,64]{1,0:T(1,128)S(1)} %bitcast.14, f32[1,128]{1,0:T(1,128)S(1)} %copy-done.3, bf16[4,256,128]{2,1,0:T(8,128)(2,1)S(1)} %all-to-all-done.1.p_ref, bf16[16,256,128]{2,1,0:T(8,128)(2,1)S(1)} %convert_element_type.32.q_ref), custom_call_target="tpu_custom_call" | custom-call | flops 2000000000 | bytes 2000000 | tf_op jit(solution)/shard_map/pallas_call | solution.py:70
  64.8 32.8 %all_to_all.16 = f32[64,16,128]{2,1,0:T(8,128)S(1)} all-to-all(f32[64,16,128]{2,1,0:T(8,128)S(1)} %bitcast.11), channel_id=1, replica_groups=mesh['aux_x'=4,'aux_y'=2,'aux_core'=2,'blk_y'=4,'blk_z'=16] {'blk_y','au..., dimensions={0} | all-to-all | bytes 1048576 | tf_op jit(solution)/shard_map/all_to_all | solution.py:96
  97.6 0.7 reduce_sum.9
  (1 shorter events, 0.0 us)
Async XLA Ops:
  24.0 37.0 %all-to-all-start.1 = ((bf16[4,256,128]{2,1,0:T(8,128)(2,1)}), bf16[4,256,128]{2,1,0:T(8,128)(2,1)S(1)}, u32[]{:S(2)}, u32[]{:S(2)}) async-start(bf16[4,256,128]{2,1,0:T(8,128)(2,1)} %broadcast_in_dim.11), calls=%async_computation.1 | async-start | bytes 524288 | tf_op jit(solution)/shard_map/all_to_all | solution.py:91
  60.8 0.8 copy-start
  60.8 0.8 copy-start.3
  61.1 0.7 copy-start.1
  61.1 0.7 copy-start.2

commit v8 on v7

--- a/solution.py
+++ b/solution.py
@@ -8,6 +8,7 @@
 AUX = ("aux_x", "aux_y", "aux_core")
 NP = 4
 NZ = 16
+RINGS = [list(range(NZ)), list(range(2 * NZ - 1, NZ - 1, -1))]
 SCALE = 2.0**14
 V = 128
 AB = 128
@@ -38,7 +39,8 @@
         block = jnp.where(live(p_index[s]), p_ref[s], zero) * (1 / SCALE)
         pcat[:, s * V : (s + 1) * V] = block * 2
         pcat_t[s * V : (s + 1) * V, :] = block.T
-    q_index = [h * NZ + k for k in range(NZ)]
+    core = lax.axis_index("aux_core")
+    q_index = [h * NZ + jnp.where(core == 0, k, NZ - 1 - k) for k in range(NZ)]
     qs, ts = [], []
     for c in range(0, NZ, 2):
         block = jnp.concatenate([jnp.where(live(q_index[c + t]), q_ref[c + t], zero) for t in range(2)], axis=1)
@@ -90,7 +92,7 @@
     own = lax.all_to_all(b_tensor[0], AUX, 0, 0, tiled=True).reshape(1, NA, V)
     p_blocks = lax.all_to_all(jnp.broadcast_to(own, (NP, NA, V)), "blk_y", 0, 0, tiled=True)
     sent = (own.astype(jnp.float32) * SCALE).astype(jnp.float16)
-    line = lax.all_gather(sent, "blk_z", axis=0, tiled=True)
+    line = lax.all_gather(sent, ("aux_core", "blk_z"), axis=0, tiled=True, axis_index_groups=RINGS)
     scalars = (significance[:, 0, :].T, pair_keep[0], occ_energy.T, virt_energy)
     part = pair_terms(scalars, p_blocks, line.astype(jnp.bfloat16))
     back = lax.all_to_all(part.reshape(64, 16, V), ("blk_y",) + AUX, 0, 0, tiled=True)

time: 98.7 us -> 98.7 us (level)
  no operation moved by 1% of the time
where the time goes in v8:
time: 98.7 us; the launch traced here: 98.3 us
  blocking collectives  89.5 us (91%)
  starting transfers between devices  3.4 us (3%)
  Pallas kernels  3.03 us (3%)
  local copies, waits for them, and re-layouts  1.4 us (1%)
    all_to_all x1, blocking collectives, on_device(): lax.all_to_all(part.reshape(64, 16, V), ('blk_y',) + AUX, 0, 0, tiled=True)  33.6 us
    all_gather x1, blocking collectives, on_device(): lax.all_gather(sent, ('aux_core', 'blk_z'), axis=0, tiled=True, axis_inde...  32.6 us
    all_to_all x1, blocking collectives, on_device(): own = lax.all_to_all(b_tensor[0], AUX, 0, 0, tiled=True).reshape(1, NA, V)  23.3 us
    all_to_all x1, starting transfers between devices, on_device(): lax.all_to_all(jnp.broadcast_to(own, (NP, NA, V)), 'blk_y', 0, 0, tiled=T...  3.4 us
    pallas_call x1, Pallas kernels, pair_terms(): pl.pallas_call(pair_kernel, out_shape=jax.ShapeDtypeStruct((NP, 16, 16, V...  3.03 us
  transfers between devices with their start and end apart: 1, of which 0 were waited for; matrix products, arithmetic and copies ran while one was open for 0% of the time, Pallas kernels for 0%

profile of v8, /device:TPU:1, one launch (start us, length us, event | category | flops | bytes accessed | tf_op | source)
XLA Modules:
  0.0 98.3 jit_solution(6639235369374080299)
XLA Ops:
  0.0 23.3 %all_to_all.15 = bf16[16,16,128]{2,1,0:T(8,128)(2,1)S(1)} all-to-all(bf16[16,16,128]{2,1,0:T(8,128)(2,1)} %bitcast.18), channel_id=1, replica_groups=mesh['aux_x'=4,'aux_y'=2,'aux_core'=2,'blk_y'=4,'blk_z'=16] {'aux_x','au..., dimensions={0} | all-to-all | bytes 131072 | tf_op jit(solution)/shard_map/all_to_all | solution.py:92
  23.3 0.7 broadcast_in_dim.11
  24.0 3.4 %all-to-all-start.1 = ((bf16[4,256,128]{2,1,0:T(8,128)(2,1)}), bf16[4,256,128]{2,1,0:T(8,128)(2,1)S(1)}, u32[]{:S(2)}, u32[]{:S(2)}) async-start(bf16[4,256,128]{2,1,0:T(8,128)(2,1)} %broadcast_in_dim.11), calls=%async_computation.1 | async-start | bytes 524288 | tf_op jit(solution)/shard_map/all_to_all | solution.py:93
  27.5 32.6 %all-gather.1 = f16[16,256,128]{2,1,0:T(8,128)(2,1)S(1)} all-gather(f16[1,256,128]{2,1,0:T(8,128)(2,1)S(1)} %bitcast.17), channel_id=1, replica_groups={{0,1,2,3,4,5,6,7,8,9,10,11,12,13,14,15},{79,78,77,76,75,74,73,72,71,70,..., dimensions={0}, use_global_device_ids=true | all-gather | bytes 1114112 | tf_op jit(solution)/shard_map/all_gather | solution.py:95
  60.1 0.0 copy-start
  60.1 0.0 copy-start.3
  60.1 0.2 convert_element_type.32.q_ref
  60.3 0.0 all-to-all-done.1.p_ref
  60.3 0.0 copy-start.1
  60.3 0.0 copy-start.2
  60.3 0.5 copy-done
  60.9 0.0 copy-done.3
  60.9 0.1 copy-done.1
  61.0 0.0 copy-done.2
  61.0 3.0 %shard_map.55 = f32[4,16,16,128]{3,2,1,0:T(8,128)S(1)} custom-call(s32[2,64]{1,0:T(2,128)S(1)} %bitcast.13, s32[64,64]{1,0:T(8,128)S(1)} %bitcast.12, f32[1,64]{1,0:T(1,128)S(1)} %bitcast.14, f32[1,128]{1,0:T(1,128)S(1)} %copy-done.3, bf16[4,256,128]{2,1,0:T(8,128)(2,1)S(1)} %all-to-all-done.1.p_ref, bf16[16,256,128]{2,1,0:T(8,128)(2,1)S(1)} %convert_element_type.32.q_ref), custom_call_target="tpu_custom_call" | custom-call | flops 2000000000 | bytes 2000000 | tf_op jit(solution)/shard_map/pallas_call | solution.py:72
  64.0 33.6 %all_to_all.16 = f32[64,16,128]{2,1,0:T(8,128)S(1)} all-to-all(f32[64,16,128]{2,1,0:T(8,128)S(1)} %bitcast.11), channel_id=1, replica_groups=mesh['aux_x'=4,'aux_y'=2,'aux_core'=2,'blk_y'=4,'blk_z'=16] {'blk_y','au..., dimensions={0} | all-to-all | bytes 1048576 | tf_op jit(solution)/shard_map/all_to_all | solution.py:98
  97.6 0.7 reduce_sum.9
  (1 shorter events, 0.0 us)
Async XLA Ops:
  24.0 36.3 %all-to-all-start.1 = ((bf16[4,256,128]{2,1,0:T(8,128)(2,1)}), bf16[4,256,128]{2,1,0:T(8,128)(2,1)S(1)}, u32[]{:S(2)}, u32[]{:S(2)}) async-start(bf16[4,256,128]{2,1,0:T(8,128)(2,1)} %broadcast_in_dim.11), calls=%async_computation.1 | async-start | bytes 524288 | tf_op jit(solution)/shard_map/all_to_all | solution.py:93
  60.1 0.8 copy-start
  60.1 0.8 copy-start.3
  60.3 0.7 copy-start.1
  60.3 0.7 copy-start.2

commit v9 on v7

--- a/solution.py
+++ b/solution.py
@@ -93,8 +93,12 @@
     line = lax.all_gather(sent, "blk_z", axis=0, tiled=True)
     scalars = (significance[:, 0, :].T, pair_keep[0], occ_energy.T, virt_energy)
     part = pair_terms(scalars, p_blocks, line.astype(jnp.bfloat16))
-    back = lax.all_to_all(part.reshape(64, 16, V), ("blk_y",) + AUX, 0, 0, tiled=True)
-    return back.reshape(NP, 16, 16, V).sum(axis=0)[None]
+    back = lax.all_to_all(part.reshape(32, 32, V), ("blk_y",) + AUX[:2], 0, 0, tiled=True)
+    total = back.reshape(NP, 8, 2, 16, V).sum(axis=0)
+    core = lax.axis_index("aux_core")
+    got = lax.ppermute(jnp.where(core == 0, total[:, 1], total[:, 0]), "aux_core", [(0, 1), (1, 0)])
+    place = lax.broadcasted_iota(jnp.int32, total.shape, 1)
+    return jnp.where(place == core, total, got[:, None]).reshape(1, 16, 16, V)
 
 
 def solution(mesh):

time: 98.7 us -> 98.9 us (level)
  blocking collectives: 89.5 us -> 56.7 us
  starting transfers between devices: 3.4 us -> 22.3 us
  waiting for transfers between devices: 0.01 us -> 13 us
    all_to_all x1 -> x0, blocking collectives: 32.8 us -> none  [on_device(): lax.all_to_all(part.reshape(64, 16, V), ('blk_y',) + AUX, 0, 0, tiled=True)]
    all_to_all x0 -> x1, waiting for transfers between devices: none -> 12.2 us  [on_device(): lax.all_to_all(part.reshape(32, 32, V), ('blk_y',) + AUX[:2], 0, 0, tiled...]
    ppermute x0 -> x1, starting transfers between devices: none -> 10.9 us  [on_device(): lax.ppermute(jnp.where(core == 0, total[:, 1], total[:, 0]), 'aux_core',...]
    all_to_all x0 -> x1, starting transfers between devices: none -> 7.95 us  [on_device(): lax.all_to_all(part.reshape(32, 32, V), ('blk_y',) + AUX[:2], 0, 0, tiled...]
  transfers between devices with their start and end apart: 1 -> 3, of which waited for: 0 -> 2; matrix products, arithmetic and copies ran while one was open for 0% -> 0% of each run, Pallas kernels for 0% -> 0%
where the time goes in v9:
time: 98.9 us; the launch traced here: 98.5 us
  blocking collectives  56.7 us (57%)
  starting transfers between devices  22.3 us (23%)
  waiting for transfers between devices  13 us (13%)
  Pallas kernels  3.84 us (4%)
  local copies, waits for them, and re-layouts  1.51 us (2%)
  other arithmetic  1.03 us (1%)
    all_gather x1, blocking collectives, on_device(): line = lax.all_gather(sent, 'blk_z', axis=0, tiled=True)  33.4 us
    all_to_all x1, blocking collectives, on_device(): own = lax.all_to_all(b_tensor[0], AUX, 0, 0, tiled=True).reshape(1, NA, V)  23.3 us
    all_to_all x1, waiting for transfers between devices, on_device(): lax.all_to_all(part.reshape(32, 32, V), ('blk_y',) + AUX[:2], 0, 0, tiled...  12.2 us
    ppermute x1, starting transfers between devices, on_device(): lax.ppermute(jnp.where(core == 0, total[:, 1], total[:, 0]), 'aux_core',...  10.9 us
    all_to_all x1, starting transfers between devices, on_device(): lax.all_to_all(part.reshape(32, 32, V), ('blk_y',) + AUX[:2], 0, 0, tiled...  7.95 us
    pallas_call x1, Pallas kernels, pair_terms(): pl.pallas_call(pair_kernel, out_shape=jax.ShapeDtypeStruct((NP, 16, 16, V...  3.84 us
    all_to_all x1, starting transfers between devices, on_device(): lax.all_to_all(jnp.broadcast_to(own, (NP, NA, V)), 'blk_y', 0, 0, tiled=T...  3.4 us
  transfers between devices with their start and end apart: 3, of which 2 were waited for; matrix products, arithmetic and copies ran while one was open for 0% of the time, Pallas kernels for 0%

profile of v9, /device:TPU:1, one launch (start us, length us, event | category | flops | bytes accessed | tf_op | source)
XLA Modules:
  0.0 98.5 jit_solution(8217039065774881567)
XLA Ops:
  0.0 23.3 %all_to_all.15 = bf16[16,16,128]{2,1,0:T(8,128)(2,1)S(1)} all-to-all(bf16[16,16,128]{2,1,0:T(8,128)(2,1)} %bitcast.26), channel_id=1, replica_groups=mesh['aux_x'=4,'aux_y'=2,'aux_core'=2,'blk_y'=4,'blk_z'=16] {'aux_x','au..., dimensions={0} | all-to-all | bytes 131072 | tf_op jit(solution)/shard_map/all_to_all | solution.py:90
  23.3 0.7 broadcast_in_dim.19
  24.0 3.4 %all-to-all-start.1 = ((bf16[4,256,128]{2,1,0:T(8,128)(2,1)}), bf16[4,256,128]{2,1,0:T(8,128)(2,1)S(1)}, u32[]{:S(2)}, u32[]{:S(2)}) async-start(bf16[4,256,128]{2,1,0:T(8,128)(2,1)} %broadcast_in_dim.19), calls=%async_computation.1 | async-start | bytes 524288 | tf_op jit(solution)/shard_map/all_to_all | solution.py:91
  27.5 33.4 %all-gather.1 = f16[16,256,128]{2,1,0:T(8,128)(2,1)S(1)} all-gather(f16[1,256,128]{2,1,0:T(8,128)(2,1)S(1)} %bitcast.25), channel_id=1, replica_groups=mesh['aux_x'=4,'aux_y'=2,'aux_core'=2,'blk_y'=4,'blk_z'=16] {'blk_z'}, dimensions={0}, use_global_device_ids=true | all-gather | bytes 1114112 | tf_op jit(solution)/shard_map/all_gather | solution.py:93
  60.9 0.0 copy-start
  60.9 0.0 copy-start.3
  60.9 0.2 convert_element_type.32.q_ref
  61.1 0.0 all-to-all-done.1.p_ref
  61.1 0.0 copy-start.1
  61.1 0.0 copy-start.2
  61.1 0.5 copy-done
  61.6 0.0 copy-done.3
  61.6 0.1 copy-done.1
  61.8 0.0 copy-done.2
  61.8 3.8 %shard_map.55 = f32[4,16,16,128]{3,2,1,0:T(8,128)} custom-call(s32[2,64]{1,0:T(2,128)S(1)} %bitcast.19, s32[64,64]{1,0:T(8,128)S(1)} %bitcast.18, f32[1,64]{1,0:T(1,128)S(1)} %bitcast.20, f32[1,128]{1,0:T(1,128)S(1)} %copy-done.3, bf16[4,256,128]{2,1,0:T(8,128)(2,1)S(1)} %all-to-all-done.1.p_ref, bf16[16,256,128]{2,1,0:T(8,128)(2,1)S(1)} %convert_element_type.32.q_ref), custom_call_target="tpu_custom_call" | custom-call | flops 2000000000 | bytes 2000000 | tf_op jit(solution)/shard_map/pallas_call | solution.py:70
  65.6 8.0 %all-to-all-start.2 = ((f32[32,32,128]{2,1,0:T(8,128)}), f32[32,32,128]{2,1,0:T(8,128)S(1)}, u32[]{:S(2)}, u32[]{:S(2)}) async-start(f32[32,32,128]{2,1,0:T(8,128)} %bitcast.7), calls=%async_computation.2 | async-start | bytes 1048576 | tf_op jit(solution)/shard_map/all_to_all | solution.py:96
  73.6 12.2 %all-to-all-done.2 = f32[32,32,128]{2,1,0:T(8,128)S(1)} async-done(((f32[32,32,128]{2,1,0:T(8,128)}), f32[32,32,128]{2,1,0:T(8,128)S(1)}, u32[]{:S(2)}, u32[]{:S(2)}) %all-to-all-start.2) | async-done | bytes 524320 | tf_op jit(solution)/shard_map/all_to_all | solution.py:96
  85.9 10.9 %collective-permute-start = (f32[8,16,128]{2,1,0:T(8,128)S(1)}, f32[8,16,128]{2,1,0:T(8,128)S(1)}, u32[]{:S(2)}, u32[]{:S(2)}) collective-permute-start(f32[8,16,128]{2,1,0:T(8,128)S(1)} %fusion), channel_id=1, source_target_pairs={{0,64},{64,0},{1,65},{65,1},{2,66},{66,2},{3,67},{67,3},{4,68},{68... | collective-permute-start | bytes 196616 | tf_op jit(solution)/shard_map/ppermute | solution.py:99
  96.9 0.1 iota.12
  96.9 0.8 collective-permute-done
  97.7 0.7 bitcast_select_fusion
  (6 shorter events, 0.1 us)
Async XLA Ops:
  24.0 37.0 %all-to-all-start.1 = ((bf16[4,256,128]{2,1,0:T(8,128)(2,1)}), bf16[4,256,128]{2,1,0:T(8,128)(2,1)S(1)}, u32[]{:S(2)}, u32[]{:S(2)}) async-start(bf16[4,256,128]{2,1,0:T(8,128)(2,1)} %broadcast_in_dim.19), calls=%async_computation.1 | async-start | bytes 524288 | tf_op jit(solution)/shard_map/all_to_all | solution.py:91
  60.9 0.8 copy-start
  60.9 0.8 copy-start.3
  61.1 0.7 copy-start.1
  61.1 0.7 copy-start.2
  65.6 20.2 %all-to-all-start.2 = ((f32[32,32,128]{2,1,0:T(8,128)}), f32[32,32,128]{2,1,0:T(8,128)S(1)}, u32[]{:S(2)}, u32[]{:S(2)}) async-start(f32[32,32,128]{2,1,0:T(8,128)} %bitcast.7), calls=%async_computation.2 | async-start | bytes 1048576 | tf_op jit(solution)/shard_map/all_to_all | solution.py:96
  85.9 11.8 %collective-permute-start = (f32[8,16,128]{2,1,0:T(8,128)S(1)}, f32[8,16,128]{2,1,0:T(8,128)S(1)}, u32[]{:S(2)}, u32[]{:S(2)}) collective-permute-start(f32[8,16,128]{2,1,0:T(8,128)S(1)} %fusion), channel_id=1, source_target_pairs={{0,64},{64,0},{1,65},{65,1},{2,66},{66,2},{3,67},{67,3},{4,68},{68... | collective-permute-start | bytes 196616 | tf_op jit(solution)/shard_map/ppermute | solution.py:99

commit v10 on v9

--- a/solution.py
+++ b/solution.py
@@ -14,7 +14,7 @@
 NA = 256
 
 
-def pair_kernel(sig_hbm, keep_hbm, occ_hbm, virt, p_ref, q_ref, out, pcat, pcat_t, vb, sig, keep, occ, done):
+def pair_kernel(sig_hbm, keep_hbm, occ_hbm, virt, p_ref, q_ref, out, here, pcat, pcat_t, vb, sig, keep, occ, done):
     copies = [
         pltpu.make_async_copy(src, dst, done.at[i])
         for i, (src, dst) in enumerate(((sig_hbm, sig), (keep_hbm, keep), (occ_hbm, occ)))
@@ -38,6 +38,8 @@
         block = jnp.where(live(p_index[s]), p_ref[s], zero) * (1 / SCALE)
         pcat[:, s * V : (s + 1) * V] = block * 2
         pcat_t[s * V : (s + 1) * V, :] = block.T
+    place = lax.broadcasted_iota(jnp.int32, here.shape, 1)
+    here[...] = (place == lax.axis_index("aux_core")).astype(jnp.int32)
     q_index = [h * NZ + k for k in range(NZ)]
     qs, ts = [], []
     for c in range(0, NZ, 2):
@@ -69,9 +71,12 @@
     vmem = pl.BlockSpec(memory_space=pltpu.VMEM)
     return pl.pallas_call(
         pair_kernel,
-        out_shape=jax.ShapeDtypeStruct((NP, 16, 16, V), jnp.float32),
+        out_shape=(
+            jax.ShapeDtypeStruct((NP, 16, 16, V), jnp.float32),
+            jax.ShapeDtypeStruct((8, 2, 16, V), jnp.int32),
+        ),
         in_specs=[hbm] * 3 + [vmem] * 3,
-        out_specs=vmem,
+        out_specs=(vmem, vmem),
         scratch_shapes=[
             pltpu.VMEM((NA, NP * V), jnp.bfloat16),
             pltpu.VMEM((NP * V, NA), jnp.bfloat16),
@@ -92,13 +97,11 @@
     sent = (own.astype(jnp.float32) * SCALE).astype(jnp.float16)
     line = lax.all_gather(sent, "blk_z", axis=0, tiled=True)
     scalars = (significance[:, 0, :].T, pair_keep[0], occ_energy.T, virt_energy)
-    part = pair_terms(scalars, p_blocks, line.astype(jnp.bfloat16))
+    part, here = pair_terms(scalars, p_blocks, line.astype(jnp.bfloat16))
     back = lax.all_to_all(part.reshape(32, 32, V), ("blk_y",) + AUX[:2], 0, 0, tiled=True)
     total = back.reshape(NP, 8, 2, 16, V).sum(axis=0)
-    core = lax.axis_index("aux_core")
-    got = lax.ppermute(jnp.where(core == 0, total[:, 1], total[:, 0]), "aux_core", [(0, 1), (1, 0)])
-    place = lax.broadcasted_iota(jnp.int32, total.shape, 1)
-    return jnp.where(place == core, total, got[:, None]).reshape(1, 16, 16, V)
+    got = lax.ppermute(jnp.where(here[:, 0] > 0, total[:, 1], total[:, 0]), "aux_core", [(0, 1), (1, 0)])
+    return jnp.where(here > 0, total, got[:, None]).reshape(1, 16, 16, V)
 
 
 def solution(mesh):

time: 98.9 us -> 97.8 us (0.989)
  blocking collectives: 56.7 us -> 76.7 us
  waiting for transfers between devices: 13 us -> 0.88 us
  starting transfers between devices: 22.3 us -> 14.3 us
    all_to_all x0 -> x1, blocking collectives: none -> 20 us  [on_device(): lax.all_to_all(part.reshape(32, 32, V), ('blk_y',) + AUX[:2], 0, 0, tiled...]
    all_to_all x1 -> x0, waiting for transfers between devices: 12.2 us -> none  [on_device(): lax.all_to_all(part.reshape(32, 32, V), ('blk_y',) + AUX[:2], 0, 0, tiled...]
    all_to_all x1 -> x0, starting transfers between devices: 7.95 us -> none  [on_device(): lax.all_to_all(part.reshape(32, 32, V), ('blk_y',) + AUX[:2], 0, 0, tiled...]
  transfers between devices with their start and end apart: 3 -> 2, of which waited for: 2 -> 1; matrix products, arithmetic and copies ran while one was open for 0% -> 0% of each run, Pallas kernels for 0% -> 0%
where the time goes in v10:
time: 97.8 us; the launch traced here: 97.4 us
  blocking collectives  76.7 us (78%)
  starting transfers between devices  14.3 us (15%)
  Pallas kernels  3.06 us (3%)
  local copies, waits for them, and re-layouts  1.41 us (1%)
    all_gather x1, blocking collectives, on_device(): line = lax.all_gather(sent, 'blk_z', axis=0, tiled=True)  33.4 us
    all_to_all x1, blocking collectives, on_device(): own = lax.all_to_all(b_tensor[0], AUX, 0, 0, tiled=True).reshape(1, NA, V)  23.3 us
    all_to_all x1, blocking collectives, on_device(): lax.all_to_all(part.reshape(32, 32, V), ('blk_y',) + AUX[:2], 0, 0, tiled...  20 us
    ppermute x1, starting transfers between devices, on_device(): lax.ppermute(jnp.where(here[:, 0] > 0, total[:, 1], total[:, 0]), 'aux_co...  10.9 us
    all_to_all x1, starting transfers between devices, on_device(): lax.all_to_all(jnp.broadcast_to(own, (NP, NA, V)), 'blk_y', 0, 0, tiled=T...  3.4 us
    pallas_call x1, Pallas kernels, pair_terms(): pl.pallas_call(pair_kernel, out_shape=(jax.ShapeDtypeStruct((NP, 16, 16,...  3.06 us
  transfers between devices with their start and end apart: 2, of which 1 were waited for; matrix products, arithmetic and copies ran while one was open for 0% of the time, Pallas kernels for 0%

profile of v10, /device:TPU:1, one launch (start us, length us, event | category | flops | bytes accessed | tf_op | source)
XLA Modules:
  0.0 97.4 jit_solution(15260069104553728321)
XLA Ops:
  0.0 23.3 %all_to_all.15 = bf16[16,16,128]{2,1,0:T(8,128)(2,1)S(1)} all-to-all(bf16[16,16,128]{2,1,0:T(8,128)(2,1)} %bitcast.20), channel_id=1, replica_groups=mesh['aux_x'=4,'aux_y'=2,'aux_core'=2,'blk_y'=4,'blk_z'=16] {'aux_x','au..., dimensions={0} | all-to-all | bytes 131072 | tf_op jit(solution)/shard_map/all_to_all | solution.py:95
  23.3 0.7 broadcast_in_dim.17
  24.0 3.4 %all-to-all-start.1 = ((bf16[4,256,128]{2,1,0:T(8,128)(2,1)}), bf16[4,256,128]{2,1,0:T(8,128)(2,1)S(1)}, u32[]{:S(2)}, u32[]{:S(2)}) async-start(bf16[4,256,128]{2,1,0:T(8,128)(2,1)} %broadcast_in_dim.17), calls=%async_computation.1 | async-start | bytes 524288 | tf_op jit(solution)/shard_map/all_to_all | solution.py:96
  27.5 33.4 %all-gather.1 = f16[16,256,128]{2,1,0:T(8,128)(2,1)S(1)} all-gather(f16[1,256,128]{2,1,0:T(8,128)(2,1)S(1)} %bitcast.19), channel_id=1, replica_groups=mesh['aux_x'=4,'aux_y'=2,'aux_core'=2,'blk_y'=4,'blk_z'=16] {'blk_z'}, dimensions={0}, use_global_device_ids=true | all-gather | bytes 1114112 | tf_op jit(solution)/shard_map/all_gather | solution.py:98
  60.8 0.0 copy-start
  60.9 0.0 copy-start.3
  60.9 0.2 convert_element_type.32.q_ref
  61.1 0.0 all-to-all-done.1.p_ref
  61.1 0.0 copy-start.1
  61.1 0.0 copy-start.2
  61.1 0.5 copy-done
  61.6 0.0 copy-done.3
  61.6 0.1 copy-done.1
  61.8 0.0 copy-done.2
  61.8 3.1 %shard_map.55 = (f32[4,16,16,128]{3,2,1,0:T(8,128)S(1)}, s32[8,2,16,128]{3,2,1,0:T(8,128)S(1)}) custom-call(s32[2,64]{1,0:T(2,128)S(1)} %bitcast.15, s32[64,64]{1,0:T(8,128)S(1)} %bitcast.14, f32[1,64]{1,0:T(1,128)S(1)} %bitcast.16, f32[1,128]{1,0:T(1,128)S(1)} %copy-done.3, bf16[4,256,128]{2,1,0:T(8,128)(2,1)S(1)} %all-to-all-done.1.p_ref, ...), custom_call_target="tpu_custom_call" | custom-call | flops 2000000000 | bytes 2000000 | tf_op jit(solution)/shard_map/pallas_call | solution.py:72
  64.8 20.0 %all_to_all.16 = f32[32,32,128]{2,1,0:T(8,128)S(1)} all-to-all(f32[32,32,128]{2,1,0:T(8,128)S(1)} %bitcast.13), channel_id=1, replica_groups=mesh['aux_x'=4,'aux_y'=2,'aux_core'=2,'blk_y'=4,'blk_z'=16] {'blk_y','au..., dimensions={0} | all-to-all | bytes 1048576 | tf_op jit(solution)/shard_map/all_to_all | solution.py:101
  84.9 10.9 %collective-permute-start = (f32[8,16,128]{2,1,0:T(8,128)S(1)}, f32[8,16,128]{2,1,0:T(8,128)S(1)}, u32[]{:S(2)}, u32[]{:S(2)}) collective-permute-start(f32[8,16,128]{2,1,0:T(8,128)S(1)} %fusion), channel_id=1, source_target_pairs={{0,64},{64,0},{1,65},{65,1},{2,66},{66,2},{3,67},{67,3},{4,68},{68... | collective-permute-start | bytes 196616 | tf_op jit(solution)/shard_map/ppermute | solution.py:103
  95.8 0.9 collective-permute-done
  96.7 0.7 compare_select_fusion
  (3 shorter events, 0.1 us)
Async XLA Ops:
  24.0 37.0 %all-to-all-start.1 = ((bf16[4,256,128]{2,1,0:T(8,128)(2,1)}), bf16[4,256,128]{2,1,0:T(8,128)(2,1)S(1)}, u32[]{:S(2)}, u32[]{:S(2)}) async-start(bf16[4,256,128]{2,1,0:T(8,128)(2,1)} %broadcast_in_dim.17), calls=%async_computation.1 | async-start | bytes 524288 | tf_op jit(solution)/shard_map/all_to_all | solution.py:96
  60.8 0.8 copy-start
  60.9 0.8 copy-start.3
  61.1 0.7 copy-start.1
  61.1 0.7 copy-start.2
  84.9 11.8 %collective-permute-start = (f32[8,16,128]{2,1,0:T(8,128)S(1)}, f32[8,16,128]{2,1,0:T(8,128)S(1)}, u32[]{:S(2)}, u32[]{:S(2)}) collective-permute-start(f32[8,16,128]{2,1,0:T(8,128)S(1)} %fusion), channel_id=1, source_target_pairs={{0,64},{64,0},{1,65},{65,1},{2,66},{66,2},{3,67},{67,3},{4,68},{68... | collective-permute-start | bytes 196616 | tf_op jit(solution)/shard_map/ppermute | solution.py:103

commit v11 on v10

--- a/solution.py
+++ b/solution.py
@@ -14,7 +14,7 @@
 NA = 256
 
 
-def pair_kernel(sig_hbm, keep_hbm, occ_hbm, virt, p_ref, q_ref, out, here, pcat, pcat_t, vb, sig, keep, occ, done):
+def pair_kernel(sig_hbm, keep_hbm, occ_hbm, virt, p0, p1, p2, p3, q_ref, out, here, pcat, pcat_t, vb, sig, keep, occ, done):
     copies = [
         pltpu.make_async_copy(src, dst, done.at[i])
         for i, (src, dst) in enumerate(((sig_hbm, sig), (keep_hbm, keep), (occ_hbm, occ)))
@@ -33,9 +33,9 @@
     def live(orbital):
         return jnp.where(rows < AB, sig[0, orbital], sig[1, orbital]) > 0
 
-    p_index = [s * NZ + w for s in range(NP)]
+    p_index = [lax.rem(h + s, NP) * NZ + w for s in range(NP)]
     for s in range(NP):
-        block = jnp.where(live(p_index[s]), p_ref[s], zero) * (1 / SCALE)
+        block = jnp.where(live(p_index[s]), (p0, p1, p2, p3)[s][0], zero) * (1 / SCALE)
         pcat[:, s * V : (s + 1) * V] = block * 2
         pcat_t[s * V : (s + 1) * V, :] = block.T
     place = lax.broadcasted_iota(jnp.int32, here.shape, 1)
@@ -63,7 +63,7 @@
     gammas = jnp.dot(jnp.concatenate(qs, axis=1), jnp.concatenate(ts, axis=0), preferred_element_type=jnp.float32)
     for s in range(NP):
         gamma = jnp.where(live(p_index[s]), gammas[:, s * V : (s + 1) * V], 0.0) * (1 / SCALE)
-        out[s] = gamma.reshape(16, 16, V)
+        out[lax.rem(h + s, NP)] = gamma.reshape(16, 16, V)
 
 
 def pair_terms(scalars, p_blocks, q_blocks):
@@ -75,7 +75,7 @@
             jax.ShapeDtypeStruct((NP, 16, 16, V), jnp.float32),
             jax.ShapeDtypeStruct((8, 2, 16, V), jnp.int32),
         ),
-        in_specs=[hbm] * 3 + [vmem] * 3,
+        in_specs=[hbm] * 3 + [vmem] * (2 + NP),
         out_specs=(vmem, vmem),
         scratch_shapes=[
             pltpu.VMEM((NA, NP * V), jnp.bfloat16),
@@ -88,12 +88,12 @@
         ],
         compiler_params=pltpu.CompilerParams(vmem_limit_bytes=24 * 2**20),
         cost_estimate=pl.CostEstimate(flops=2 * 10**9, bytes_accessed=2 * 10**6, transcendentals=10**6),
-    )(*scalars, p_blocks, q_blocks)
+    )(*scalars, *p_blocks, q_blocks)
 
 
 def on_device(b_tensor, significance, pair_keep, occ_energy, virt_energy):
     own = lax.all_to_all(b_tensor[0], AUX, 0, 0, tiled=True).reshape(1, NA, V)
-    p_blocks = lax.all_to_all(jnp.broadcast_to(own, (NP, NA, V)), "blk_y", 0, 0, tiled=True)
+    p_blocks = [own] + [lax.ppermute(own, "blk_y", [((i + s) % NP, i) for i in range(NP)]) for s in range(1, NP)]
     sent = (own.astype(jnp.float32) * SCALE).astype(jnp.float16)
     line = lax.all_gather(sent, "blk_z", axis=0, tiled=True)
     scalars = (significance[:, 0, :].T, pair_keep[0], occ_energy.T, virt_energy)

time: 97.8 us -> 101 us (1.033)
  starting transfers between devices: 14.3 us -> 20.5 us
  blocking collectives: 76.7 us -> 74.7 us
    ppermute x0 -> x3, starting transfers between devices: none -> 9.3 us  [on_device(): lax.ppermute(own, 'blk_y', [((i + s) % NP, i) for i in range(NP)])]
    all_to_all x1, blocking collectives: 20 us -> 15.2 us  [on_device(): lax.all_to_all(part.reshape(32, 32, V), ('blk_y',) + AUX[:2], 0, 0, tiled...]
    all_to_all x1 -> x0, starting transfers between devices: 3.4 us -> none  [on_device(): lax.all_to_all(jnp.broadcast_to(own, (NP, NA, V)), 'blk_y', 0, 0, tiled=T...]
    all_gather x1, blocking collectives: 33.4 us -> 36.2 us  [on_device(): line = lax.all_gather(sent, 'blk_z', axis=0, tiled=True)]
  transfers between devices with their start and end apart: 2 -> 4, of which waited for: 1 -> 1; matrix products, arithmetic and copies ran while one was open for 0% -> 0% of each run, Pallas kernels for 0% -> 0%
where the time goes in v11:
time: 101 us
  blocking collectives  74.7 us (74%)
  starting transfers between devices  20.5 us (20%)
  Pallas kernels  3.06 us (3%)
    all_gather x1, blocking collectives, on_device(): line = lax.all_gather(sent, 'blk_z', axis=0, tiled=True)  36.2 us
    all_to_all x1, blocking collectives, on_device(): own = lax.all_to_all(b_tensor[0], AUX, 0, 0, tiled=True).reshape(1, NA, V)  23.3 us
    all_to_all x1, blocking collectives, on_device(): lax.all_to_all(part.reshape(32, 32, V), ('blk_y',) + AUX[:2], 0, 0, tiled...  15.2 us
    ppermute x1, starting transfers between devices, on_device(): lax.ppermute(jnp.where(here[:, 0] > 0, total[:, 1], total[:, 0]), 'aux_co...  11.2 us
    ppermute x3, starting transfers between devices, on_device(): lax.ppermute(own, 'blk_y', [((i + s) % NP, i) for i in range(NP)])  9.3 us
    pallas_call x1, Pallas kernels, pair_terms(): pl.pallas_call(pair_kernel, out_shape=(jax.ShapeDtypeStruct((NP, 16, 16,...  3.06 us
  transfers between devices with their start and end apart: 4, of which 1 were waited for; matrix products, arithmetic and copies ran while one was open for 0% of the time, Pallas kernels for 0%

profile of v11, /device:TPU:1, one launch (start us, length us, event | category | flops | bytes accessed | tf_op | source)
XLA Modules:
  0.0 100.9 jit_solution(5465649839671891543)
XLA Ops:
  0.0 23.3 %all_to_all.10 = bf16[16,16,128]{2,1,0:T(8,128)(2,1)S(1)} all-to-all(bf16[16,16,128]{2,1,0:T(8,128)(2,1)} %bitcast.24), channel_id=1, replica_groups=mesh['aux_x'=4,'aux_y'=2,'aux_core'=2,'blk_y'=4,'blk_z'=16] {'aux_x','au..., dimensions={0} | all-to-all | bytes 131072 | tf_op jit(solution)/shard_map/all_to_all | solution.py:95
  23.3 1.9 %collective-permute-start.2 = (bf16[1,256,128]{2,1,0:T(8,128)(2,1)S(1)}, bf16[1,256,128]{2,1,0:T(8,128)(2,1)S(1)}, u32[]{:S(2)}, u32[]{:S(2)}) collective-permute-start(bf16[1,256,128]{2,1,0:T(8,128)(2,1)S(1)} %bitcast.15), channel_id=1, source_target_pairs={{48,0},{0,16},{16,32},{32,48},{49,1},{1,17},{17,33},{33,49},{50,2}... | collective-permute-start | bytes 196616 | tf_op jit(solution)/shard_map/ppermute | solution.py:96
  25.2 1.9 %collective-permute-start.1 = (bf16[1,256,128]{2,1,0:T(8,128)(2,1)S(1)}, bf16[1,256,128]{2,1,0:T(8,128)(2,1)S(1)}, u32[]{:S(2)}, u32[]{:S(2)}) collective-permute-start(bf16[1,256,128]{2,1,0:T(8,128)(2,1)S(1)} %bitcast.16), channel_id=1, source_target_pairs={{32,0},{48,16},{0,32},{16,48},{33,1},{49,17},{1,33},{17,49},{34,2}... | collective-permute-start | bytes 196616 | tf_op jit(solution)/shard_map/ppermute | solution.py:96
  27.2 5.5 %collective-permute-start = (bf16[1,256,128]{2,1,0:T(8,128)(2,1)S(1)}, bf16[1,256,128]{2,1,0:T(8,128)(2,1)S(1)}, u32[]{:S(2)}, u32[]{:S(2)}) collective-permute-start(bf16[1,256,128]{2,1,0:T(8,128)(2,1)S(1)} %bitcast.17), channel_id=1, source_target_pairs={{16,0},{32,16},{48,32},{0,48},{17,1},{33,17},{49,33},{1,49},{18,2}... | collective-permute-start | bytes 196616 | tf_op jit(solution)/shard_map/ppermute | solution.py:96
  32.7 36.2 %all-gather.1 = f16[16,256,128]{2,1,0:T(8,128)(2,1)S(1)} all-gather(f16[1,256,128]{2,1,0:T(8,128)(2,1)S(1)} %multiply_convert_fusion), channel_id=1, replica_groups=mesh['aux_x'=4,'aux_y'=2,'aux_core'=2,'blk_y'=4,'blk_z'=16] {'blk_z'}, dimensions={0}, use_global_device_ids=true | all-gather | bytes 1114112 | tf_op jit(solution)/shard_map/all_gather | solution.py:98
  68.9 0.0 copy-start
  68.9 0.0 copy-start.3
  68.9 0.2 convert_element_type.27.q_ref
  69.1 0.0 collective-permute-done.2.p3
  69.1 0.0 collective-permute-done.1.p2
  69.1 0.0 collective-permute-done.p1
  69.1 0.0 copy-start.1
  69.1 0.0 copy-start.2
  69.1 0.5 copy-done
  69.6 0.0 copy-done.3
  69.6 0.2 copy-done.1
  69.8 0.0 copy-done.2
  69.8 3.1 %shard_map.55 = (f32[4,16,16,128]{3,2,1,0:T(8,128)S(1)}, s32[8,2,16,128]{3,2,1,0:T(8,128)S(1)}) custom-call(s32[2,64]{1,0:T(2,128)S(1)} %bitcast.21, s32[64,64]{1,0:T(8,128)S(1)} %bitcast.20, f32[1,64]{1,0:T(1,128)S(1)} %bitcast.22, f32[1,128]{1,0:T(1,128)S(1)} %copy-done.3, bf16[1,256,128]{2,1,0:T(8,128)(2,1)S(1)} %bitcast.19, ...), custom_call_target="tpu_custom_call" | custom-call | flops 2000000000 | bytes 2000000 | tf_op jit(solution)/shard_map/pallas_call | solution.py:72
  72.9 15.2 %all_to_all.11 = f32[32,32,128]{2,1,0:T(8,128)S(1)} all-to-all(f32[32,32,128]{2,1,0:T(8,128)S(1)} %bitcast.14), channel_id=1, replica_groups=mesh['aux_x'=4,'aux_y'=2,'aux_core'=2,'blk_y'=4,'blk_z'=16] {'blk_y','au..., dimensions={0} | all-to-all | bytes 1048576 | tf_op jit(solution)/shard_map/all_to_all | solution.py:101
  88.1 11.2 %collective-permute-start.3 = (f32[8,16,128]{2,1,0:T(8,128)S(1)}, f32[8,16,128]{2,1,0:T(8,128)S(1)}, u32[]{:S(2)}, u32[]{:S(2)}) collective-permute-start(f32[8,16,128]{2,1,0:T(8,128)S(1)} %fusion), channel_id=1, source_target_pairs={{0,64},{64,0},{1,65},{65,1},{2,66},{66,2},{3,67},{67,3},{4,68},{68... | collective-permute-start | bytes 196616 | tf_op jit(solution)/shard_map/ppermute | solution.py:103
  99.3 0.9 collective-permute-done.3
  100.2 0.7 compare_select_fusion
  (3 shorter events, 0.1 us)
Async XLA Ops:
  23.3 45.8 %collective-permute-start.2 = (bf16[1,256,128]{2,1,0:T(8,128)(2,1)S(1)}, bf16[1,256,128]{2,1,0:T(8,128)(2,1)S(1)}, u32[]{:S(2)}, u32[]{:S(2)}) collective-permute-start(bf16[1,256,128]{2,1,0:T(8,128)(2,1)S(1)} %bitcast.15), channel_id=1, source_target_pairs={{48,0},{0,16},{16,32},{32,48},{49,1},{1,17},{17,33},{33,49},{50,2}... | collective-permute-start | bytes 196616 | tf_op jit(solution)/shard_map/ppermute | solution.py:96
  25.2 43.9 %collective-permute-start.1 = (bf16[1,256,128]{2,1,0:T(8,128)(2,1)S(1)}, bf16[1,256,128]{2,1,0:T(8,128)(2,1)S(1)}, u32[]{:S(2)}, u32[]{:S(2)}) collective-permute-start(bf16[1,256,128]{2,1,0:T(8,128)(2,1)S(1)} %bitcast.16), channel_id=1, source_target_pairs={{32,0},{48,16},{0,32},{16,48},{33,1},{49,17},{1,33},{17,49},{34,2}... | collective-permute-start | bytes 196616 | tf_op jit(solution)/shard_map/ppermute | solution.py:96
  27.2 41.9 %collective-permute-start = (bf16[1,256,128]{2,1,0:T(8,128)(2,1)S(1)}, bf16[1,256,128]{2,1,0:T(8,128)(2,1)S(1)}, u32[]{:S(2)}, u32[]{:S(2)}) collective-permute-start(bf16[1,256,128]{2,1,0:T(8,128)(2,1)S(1)} %bitcast.17), channel_id=1, source_target_pairs={{16,0},{32,16},{48,32},{0,48},{17,1},{33,17},{49,33},{1,49},{18,2}... | collective-permute-start | bytes 196616 | tf_op jit(solution)/shard_map/ppermute | solution.py:96
  68.9 0.8 copy-start
  68.9 0.8 copy-start.3
  69.1 0.7 copy-start.1
  69.1 0.7 copy-start.2
  88.1 12.1 %collective-permute-start.3 = (f32[8,16,128]{2,1,0:T(8,128)S(1)}, f32[8,16,128]{2,1,0:T(8,128)S(1)}, u32[]{:S(2)}, u32[]{:S(2)}) collective-permute-start(f32[8,16,128]{2,1,0:T(8,128)S(1)} %fusion), channel_id=1, source_target_pairs={{0,64},{64,0},{1,65},{65,1},{2,66},{66,2},{3,67},{67,3},{4,68},{68... | collective-permute-start | bytes 196616 | tf_op jit(solution)/shard_map/ppermute | solution.py:103

commit v12 on v10

--- a/solution.py
+++ b/solution.py
@@ -51,11 +51,11 @@
             tiles = []
             for t in range(2):
                 p, q = p_index[s], q_index[c + t]
-                kept = keep[lax.min(p, q), lax.max(p, q)].astype(jnp.float32)
+                kept = keep[lax.min(p, q), lax.max(p, q)]
                 total = occ[0, p] + occ[0, q]
                 top = twice[t * V : (t + 1) * V, s * V : (s + 1) * V]
                 top = top - swapped[s * V : (s + 1) * V, t * V : (t + 1) * V]
-                tiles.append((kept * top / ((total - va) - vb[...])).astype(jnp.bfloat16))
+                tiles.append((kept * top / ((va - total) + vb[...])).astype(jnp.bfloat16))
             columns.append(jnp.concatenate(tiles, axis=0))
         tilde = jnp.concatenate(columns, axis=1)
         qs.append(block)
@@ -81,8 +81,8 @@
             pltpu.VMEM((NA, NP * V), jnp.bfloat16),
             pltpu.VMEM((NP * V, NA), jnp.bfloat16),
             pltpu.VMEM((V, V), jnp.float32),
-            pltpu.SMEM((2, NP * NZ), jnp.int32),
-            pltpu.SMEM((NP * NZ, NP * NZ), jnp.int32),
+            pltpu.SMEM((2, NP * NZ), jnp.float32),
+            pltpu.SMEM((NP * NZ, NP * NZ), jnp.float32),
             pltpu.SMEM((1, NP * NZ), jnp.float32),
             pltpu.SemaphoreType.DMA((3,)),
         ],
@@ -95,8 +95,14 @@
     own = lax.all_to_all(b_tensor[0], AUX, 0, 0, tiled=True).reshape(1, NA, V)
     p_blocks = lax.all_to_all(jnp.broadcast_to(own, (NP, NA, V)), "blk_y", 0, 0, tiled=True)
     sent = (own.astype(jnp.float32) * SCALE).astype(jnp.float16)
+    scalars = (
+        significance[:, 0, :].T.astype(jnp.float32),
+        pair_keep[0].astype(jnp.float32),
+        -occ_energy.T,
+        -virt_energy,
+    )
+    sent, *scalars = lax.optimization_barrier((sent, *scalars))
     line = lax.all_gather(sent, "blk_z", axis=0, tiled=True)
-    scalars = (significance[:, 0, :].T, pair_keep[0], occ_energy.T, virt_energy)
     part, here = pair_terms(scalars, p_blocks, line.astype(jnp.bfloat16))
     back = lax.all_to_all(part.reshape(32, 32, V), ("blk_y",) + AUX[:2], 0, 0, tiled=True)
     total = back.reshape(NP, 8, 2, 16, V).sum(axis=0)

time: 97.8 us -> 97.3 us (level)
  blocking collectives: 76.7 us -> 53.4 us
  starting transfers between devices: 14.3 us -> 31.9 us
  waiting for transfers between devices: 0.88 us -> 4.76 us
  local copies, waits for them, and re-layouts: 1.41 us -> 2.7 us
    all_to_all x1 -> x0, blocking collectives: 23.3 us -> none  [on_device(): own = lax.all_to_all(b_tensor[0], AUX, 0, 0, tiled=True).reshape(1, NA, V)]
    all_to_all x0 -> x1, starting transfers between devices: none -> 17.6 us  [on_device(): own = lax.all_to_all(b_tensor[0], AUX, 0, 0, tiled=True).reshape(1, NA, V)]
    all_to_all x0 -> x1, waiting for transfers between devices: none -> 3.88 us  [on_device(): own = lax.all_to_all(b_tensor[0], AUX, 0, 0, tiled=True).reshape(1, NA, V)]
    unnamed x8, local copies, waits for them, and re-layouts: 0.67 us -> 1.97 us
  transfers between devices with their start and end apart: 2 -> 3, of which waited for: 1 -> 2; matrix products, arithmetic and copies ran while one was open for 0% -> 0% of each run, Pallas kernels for 0% -> 0%
where the time goes in v12:
time: 97.3 us; the launch traced here: 96.9 us
  blocking collectives  53.4 us (55%)
  starting transfers between devices  31.9 us (33%)
  waiting for transfers between devices  4.76 us (5%)
  Pallas kernels  3.09 us (3%)
  local copies, waits for them, and re-layouts  2.7 us (3%)
    all_gather x1, blocking collectives, on_device(): line = lax.all_gather(sent, 'blk_z', axis=0, tiled=True)  33.3 us
    all_to_all x1, blocking collectives, on_device(): lax.all_to_all(part.reshape(32, 32, V), ('blk_y',) + AUX[:2], 0, 0, tiled...  20 us
    all_to_all x1, starting transfers between devices, on_device(): own = lax.all_to_all(b_tensor[0], AUX, 0, 0, tiled=True).reshape(1, NA, V)  17.6 us
    ppermute x1, starting transfers between devices, on_device(): lax.ppermute(jnp.where(here[:, 0] > 0, total[:, 1], total[:, 0]), 'aux_co...  10.9 us
    all_to_all x1, waiting for transfers between devices, on_device(): own = lax.all_to_all(b_tensor[0], AUX, 0, 0, tiled=True).reshape(1, NA, V)  3.88 us
    all_to_all x1, starting transfers between devices, on_device(): lax.all_to_all(jnp.broadcast_to(own, (NP, NA, V)), 'blk_y', 0, 0, tiled=T...  3.4 us
    pallas_call x1, Pallas kernels, pair_terms(): pl.pallas_call(pair_kernel, out_shape=(jax.ShapeDtypeStruct((NP, 16, 16,...  3.09 us
    unnamed x8, local copies, waits for them, and re-layouts  1.97 us
  transfers between devices with their start and end apart: 3, of which 2 were waited for; matrix products, arithmetic and copies ran while one was open for 0% of the time, Pallas kernels for 0%

profile of v12, /device:TPU:1, one launch (start us, length us, event | category | flops | bytes accessed | tf_op | source)
XLA Modules:
  0.0 96.9 jit_solution(10662261375391686276)
XLA Ops:
  0.0 0.0 copy-start
  0.0 17.6 %all-to-all-start = ((bf16[16,16,128]{2,1,0:T(8,128)(2,1)}), bf16[16,16,128]{2,1,0:T(8,128)(2,1)S(1)}, u32[]{:S(2)}, u32[]{:S(2)}) async-start(bf16[16,16,128]{2,1,0:T(8,128)(2,1)} %bitcast.20), calls=%async_computation | async-start | bytes 131072 | tf_op jit(solution)/shard_map/all_to_all | solution.py:95
  17.6 0.0 copy-done
  17.6 0.0 copy-start.1
  17.6 0.7 copy-done.1
  18.3 0.0 copy-start.2
  18.3 0.7 copy-done.2
  18.9 0.0 copy-start.3
  18.9 0.7 copy-done.3
  19.6 3.9 %all-to-all-done = bf16[16,16,128]{2,1,0:T(8,128)(2,1)S(1)} async-done(((bf16[16,16,128]{2,1,0:T(8,128)(2,1)}), bf16[16,16,128]{2,1,0:T(8,128)(2,1)S(1)}, u32[]{:S(2)}, u32[]{:S(2)}) %all-to-all-start) | async-done | bytes 65568 | tf_op jit(solution)/shard_map/all_to_all | solution.py:95
  23.5 0.7 broadcast_in_dim.17
  24.2 3.4 %all-to-all-start.1 = ((bf16[4,256,128]{2,1,0:T(8,128)(2,1)}), bf16[4,256,128]{2,1,0:T(8,128)(2,1)S(1)}, u32[]{:S(2)}, u32[]{:S(2)}) async-start(bf16[4,256,128]{2,1,0:T(8,128)(2,1)} %broadcast_in_dim.17), calls=%async_computation.1 | async-start | bytes 524288 | tf_op jit(solution)/shard_map/all_to_all | solution.py:96
  27.6 33.3 %all-gather.1 = f16[16,256,128]{2,1,0:T(8,128)(2,1)S(1)} all-gather(f16[1,256,128]{2,1,0:T(8,128)(2,1)S(1)} %bitcast.19), channel_id=1, replica_groups=mesh['aux_x'=4,'aux_y'=2,'aux_core'=2,'blk_y'=4,'blk_z'=16] {'blk_z'}, dimensions={0}, use_global_device_ids=true | all-gather | bytes 1114112 | tf_op jit(solution)/shard_map/all_gather | solution.py:105
  61.0 0.2 convert_element_type.52.q_ref
  61.2 0.0 all-to-all-done.1.p_ref
  61.2 3.1 %shard_map.55 = (f32[4,16,16,128]{3,2,1,0:T(8,128)S(1)}, s32[8,2,16,128]{3,2,1,0:T(8,128)S(1)}) custom-call(f32[2,64]{1,0:T(2,128)S(1)} %convert_bitcast_fusion.1.sig_hbm, f32[64,64]{1,0:T(8,128)S(1)} %convert_bitcast_fusion.keep_hbm, f32[1,64]{1,0:T(1,128)S(1)} %negate_bitcast_fusion.occ_hbm, f32[1,128]{1,0:T(1,128)S(1)} %neg.19.virt, ...), custom_call_target="tpu_custom_call" | custom-call | flops 2000000000 | bytes 2000000 | tf_op jit(solution)/shard_map/pallas_call | solution.py:72
  64.3 20.0 %all_to_all.15 = f32[32,32,128]{2,1,0:T(8,128)S(1)} all-to-all(f32[32,32,128]{2,1,0:T(8,128)S(1)} %bitcast.16), channel_id=1, replica_groups=mesh['aux_x'=4,'aux_y'=2,'aux_core'=2,'blk_y'=4,'blk_z'=16] {'blk_y','au..., dimensions={0} | all-to-all | bytes 1048576 | tf_op jit(solution)/shard_map/all_to_all | solution.py:107
  84.4 10.9 %collective-permute-start = (f32[8,16,128]{2,1,0:T(8,128)S(1)}, f32[8,16,128]{2,1,0:T(8,128)S(1)}, u32[]{:S(2)}, u32[]{:S(2)}) collective-permute-start(f32[8,16,128]{2,1,0:T(8,128)S(1)} %fusion), channel_id=1, source_target_pairs={{0,64},{64,0},{1,65},{65,1},{2,66},{66,2},{3,67},{67,3},{4,68},{68... | collective-permute-start | bytes 196616 | tf_op jit(solution)/shard_map/ppermute | solution.py:109
  95.3 0.9 collective-permute-done
  96.2 0.7 compare_select_fusion
  (7 shorter events, 0.1 us)
Async XLA Ops:
  0.0 17.6 %copy-start = (s32[1,64,64]{2,1,0:T(8,128)S(1)}, s32[1,64,64]{2,1,0:T(8,128)}, u32[]{:S(2)}) copy-start(s32[1,64,64]{2,1,0:T(8,128)} %param.7) | copy-start | bytes 49156
  0.0 23.5 %all-to-all-start = ((bf16[16,16,128]{2,1,0:T(8,128)(2,1)}), bf16[16,16,128]{2,1,0:T(8,128)(2,1)S(1)}, u32[]{:S(2)}, u32[]{:S(2)}) async-start(bf16[16,16,128]{2,1,0:T(8,128)(2,1)} %bitcast.20), calls=%async_computation | async-start | bytes 131072 | tf_op jit(solution)/shard_map/all_to_all | solution.py:95
  17.6 0.7 copy-start.1
  18.3 0.7 copy-start.2
  18.9 0.7 copy-start.3
  24.2 37.0 %all-to-all-start.1 = ((bf16[4,256,128]{2,1,0:T(8,128)(2,1)}), bf16[4,256,128]{2,1,0:T(8,128)(2,1)S(1)}, u32[]{:S(2)}, u32[]{:S(2)}) async-start(bf16[4,256,128]{2,1,0:T(8,128)(2,1)} %broadcast_in_dim.17), calls=%async_computation.1 | async-start | bytes 524288 | tf_op jit(solution)/shard_map/all_to_all | solution.py:96
  84.4 11.8 %collective-permute-start = (f32[8,16,128]{2,1,0:T(8,128)S(1)}, f32[8,16,128]{2,1,0:T(8,128)S(1)}, u32[]{:S(2)}, u32[]{:S(2)}) collective-permute-start(f32[8,16,128]{2,1,0:T(8,128)S(1)} %fusion), channel_id=1, source_target_pairs={{0,64},{64,0},{1,65},{65,1},{2,66},{66,2},{3,67},{67,3},{4,68},{68... | collective-permute-start | bytes 196616 | tf_op jit(solution)/shard_map/ppermute | solution.py:109

commit v13 on v12

--- a/solution.py
+++ b/solution.py
@@ -104,8 +104,8 @@
     sent, *scalars = lax.optimization_barrier((sent, *scalars))
     line = lax.all_gather(sent, "blk_z", axis=0, tiled=True)
     part, here = pair_terms(scalars, p_blocks, line.astype(jnp.bfloat16))
-    back = lax.all_to_all(part.reshape(32, 32, V), ("blk_y",) + AUX[:2], 0, 0, tiled=True)
-    total = back.reshape(NP, 8, 2, 16, V).sum(axis=0)
+    back = lax.all_to_all(part.reshape(NP, NA, V), "blk_y", 0, 0, tiled=True).sum(axis=0)
+    total = lax.all_to_all(back.reshape(8, 32, V), AUX[:2], 0, 0, tiled=True).reshape(8, 2, 16, V)
     got = lax.ppermute(jnp.where(here[:, 0] > 0, total[:, 1], total[:, 0]), "aux_core", [(0, 1), (1, 0)])
     return jnp.where(here > 0, total, got[:, None]).reshape(1, 16, 16, V)
 

time: 97.3 us -> 106 us (1.089)
  blocking collectives: 53.4 us -> 59.3 us
  starting transfers between devices: 31.9 us -> 34.3 us
    all_to_all x1 -> x2, blocking collectives: 20 us -> 26 us  [the longest x1 17.8 us: on_device(): lax.all_to_all(part.reshape(NP, NA, V), 'blk_y', 0, 0, tiled=True)]
    ppermute x1, starting transfers between devices: 10.9 us -> 13.4 us  [on_device(): lax.ppermute(jnp.where(here[:, 0] > 0, total[:, 1], total[:, 0]), 'aux_co...]
where the time goes in v13:
time: 106 us; the launch traced here: 105 us
  blocking collectives  59.3 us (56%)
  starting transfers between devices  34.3 us (32%)
  waiting for transfers between devices  4.76 us (4%)
  Pallas kernels  3.09 us (3%)
  local copies, waits for them, and re-layouts  2.7 us (3%)
    all_gather x1, blocking collectives, on_device(): line = lax.all_gather(sent, 'blk_z', axis=0, tiled=True)  33.3 us
    all_to_all x1, blocking collectives, on_device(): lax.all_to_all(part.reshape(NP, NA, V), 'blk_y', 0, 0, tiled=True)  17.8 us
    all_to_all x1, starting transfers between devices, on_device(): own = lax.all_to_all(b_tensor[0], AUX, 0, 0, tiled=True).reshape(1, NA, V)  17.6 us
    ppermute x1, starting transfers between devices, on_device(): lax.ppermute(jnp.where(here[:, 0] > 0, total[:, 1], total[:, 0]), 'aux_co...  13.4 us
    all_to_all x1, blocking collectives, on_device(): lax.all_to_all(back.reshape(8, 32, V), AUX[:2], 0, 0, tiled=True)  8.12 us
    all_to_all x1, waiting for transfers between devices, on_device(): own = lax.all_to_all(b_tensor[0], AUX, 0, 0, tiled=True).reshape(1, NA, V)  3.88 us
    all_to_all x1, starting transfers between devices, on_device(): lax.all_to_all(jnp.broadcast_to(own, (NP, NA, V)), 'blk_y', 0, 0, tiled=T...  3.4 us
    pallas_call x1, Pallas kernels, pair_terms(): pl.pallas_call(pair_kernel, out_shape=(jax.ShapeDtypeStruct((NP, 16, 16,...  3.09 us
  transfers between devices with their start and end apart: 3, of which 2 were waited for; matrix products, arithmetic and copies ran while one was open for 0% of the time, Pallas kernels for 0%

profile of v13, /device:TPU:1, one launch (start us, length us, event | category | flops | bytes accessed | tf_op | source)
XLA Modules:
  0.0 105.2 jit_solution(2423908633542349402)
XLA Ops:
  0.0 0.0 copy-start
  0.0 17.6 %all-to-all-start = ((bf16[16,16,128]{2,1,0:T(8,128)(2,1)}), bf16[16,16,128]{2,1,0:T(8,128)(2,1)S(1)}, u32[]{:S(2)}, u32[]{:S(2)}) async-start(bf16[16,16,128]{2,1,0:T(8,128)(2,1)} %bitcast.23), calls=%async_computation | async-start | bytes 131072 | tf_op jit(solution)/shard_map/all_to_all | solution.py:95
  17.6 0.0 copy-done
  17.6 0.0 copy-start.1
  17.6 0.7 copy-done.1
  18.3 0.0 copy-start.2
  18.3 0.7 copy-done.2
  18.9 0.0 copy-start.3
  18.9 0.7 copy-done.3
  19.6 3.9 %all-to-all-done = bf16[16,16,128]{2,1,0:T(8,128)(2,1)S(1)} async-done(((bf16[16,16,128]{2,1,0:T(8,128)(2,1)}), bf16[16,16,128]{2,1,0:T(8,128)(2,1)S(1)}, u32[]{:S(2)}, u32[]{:S(2)}) %all-to-all-start) | async-done | bytes 65568 | tf_op jit(solution)/shard_map/all_to_all | solution.py:95
  23.5 0.7 broadcast_in_dim.17
  24.2 3.4 %all-to-all-start.1 = ((bf16[4,256,128]{2,1,0:T(8,128)(2,1)}), bf16[4,256,128]{2,1,0:T(8,128)(2,1)S(1)}, u32[]{:S(2)}, u32[]{:S(2)}) async-start(bf16[4,256,128]{2,1,0:T(8,128)(2,1)} %broadcast_in_dim.17), calls=%async_computation.1 | async-start | bytes 524288 | tf_op jit(solution)/shard_map/all_to_all | solution.py:96
  27.6 33.3 %all-gather.1 = f16[16,256,128]{2,1,0:T(8,128)(2,1)S(1)} all-gather(f16[1,256,128]{2,1,0:T(8,128)(2,1)S(1)} %bitcast.22), channel_id=1, replica_groups=mesh['aux_x'=4,'aux_y'=2,'aux_core'=2,'blk_y'=4,'blk_z'=16] {'blk_z'}, dimensions={0}, use_global_device_ids=true | all-gather | bytes 1114112 | tf_op jit(solution)/shard_map/all_gather | solution.py:105
  61.0 0.2 convert_element_type.52.q_ref
  61.2 0.0 all-to-all-done.1.p_ref
  61.2 3.1 %shard_map.55 = (f32[4,16,16,128]{3,2,1,0:T(8,128)S(1)}, s32[8,2,16,128]{3,2,1,0:T(8,128)S(1)}) custom-call(f32[2,64]{1,0:T(2,128)S(1)} %convert_bitcast_fusion.1.sig_hbm, f32[64,64]{1,0:T(8,128)S(1)} %convert_bitcast_fusion.keep_hbm, f32[1,64]{1,0:T(1,128)S(1)} %negate_bitcast_fusion.occ_hbm, f32[1,128]{1,0:T(1,128)S(1)} %neg.19.virt, ...), custom_call_target="tpu_custom_call" | custom-call | flops 2000000000 | bytes 2000000 | tf_op jit(solution)/shard_map/pallas_call | solution.py:72
  64.3 17.8 %all_to_all.20 = f32[4,256,128]{2,1,0:T(8,128)S(1)} all-to-all(f32[4,256,128]{2,1,0:T(8,128)S(1)} %bitcast.17), channel_id=1, replica_groups=mesh['aux_x'=4,'aux_y'=2,'aux_core'=2,'blk_y'=4,'blk_z'=16] {'blk_y'}, dimensions={0} | all-to-all | bytes 1048576 | tf_op jit(solution)/shard_map/all_to_all | solution.py:107
  82.2 8.1 %all_to_all.21 = f32[8,32,128]{2,1,0:T(8,128)S(1)} all-to-all(f32[8,32,128]{2,1,0:T(8,128)S(1)} %bitcast.21), channel_id=1, replica_groups=mesh['aux_x'=4,'aux_y'=2,'aux_core'=2,'blk_y'=4,'blk_z'=16] {'aux_x','au..., dimensions={0} | all-to-all | bytes 262144 | tf_op jit(solution)/shard_map/all_to_all | solution.py:108
  90.3 13.4 %collective-permute-start = (f32[8,16,128]{2,1,0:T(8,128)S(1)}, f32[8,16,128]{2,1,0:T(8,128)S(1)}, u32[]{:S(2)}, u32[]{:S(2)}) collective-permute-start(f32[8,16,128]{2,1,0:T(8,128)S(1)} %fusion), channel_id=1, source_target_pairs={{0,64},{64,0},{1,65},{65,1},{2,66},{66,2},{3,67},{67,3},{4,68},{68... | collective-permute-start | bytes 196616 | tf_op jit(solution)/shard_map/ppermute | solution.py:109
  103.7 0.9 collective-permute-done
  104.6 0.7 compare_select_fusion
  (7 shorter events, 0.1 us)
Async XLA Ops:
  0.0 17.6 %copy-start = (s32[1,64,64]{2,1,0:T(8,128)S(1)}, s32[1,64,64]{2,1,0:T(8,128)}, u32[]{:S(2)}) copy-start(s32[1,64,64]{2,1,0:T(8,128)} %param.7) | copy-start | bytes 49156
  0.0 23.5 %all-to-all-start = ((bf16[16,16,128]{2,1,0:T(8,128)(2,1)}), bf16[16,16,128]{2,1,0:T(8,128)(2,1)S(1)}, u32[]{:S(2)}, u32[]{:S(2)}) async-start(bf16[16,16,128]{2,1,0:T(8,128)(2,1)} %bitcast.23), calls=%async_computation | async-start | bytes 131072 | tf_op jit(solution)/shard_map/all_to_all | solution.py:95
  17.6 0.7 copy-start.1
  18.3 0.7 copy-start.2
  18.9 0.7 copy-start.3
  24.2 37.0 %all-to-all-start.1 = ((bf16[4,256,128]{2,1,0:T(8,128)(2,1)}), bf16[4,256,128]{2,1,0:T(8,128)(2,1)S(1)}, u32[]{:S(2)}, u32[]{:S(2)}) async-start(bf16[4,256,128]{2,1,0:T(8,128)(2,1)} %broadcast_in_dim.17), calls=%async_computation.1 | async-start | bytes 524288 | tf_op jit(solution)/shard_map/all_to_all | solution.py:96
  90.3 14.2 %collective-permute-start = (f32[8,16,128]{2,1,0:T(8,128)S(1)}, f32[8,16,128]{2,1,0:T(8,128)S(1)}, u32[]{:S(2)}, u32[]{:S(2)}) collective-permute-start(f32[8,16,128]{2,1,0:T(8,128)S(1)} %fusion), channel_id=1, source_target_pairs={{0,64},{64,0},{1,65},{65,1},{2,66},{66,2},{3,67},{67,3},{4,68},{68... | collective-permute-start | bytes 196616 | tf_op jit(solution)/shard_map/ppermute | solution.py:109

commit v14 on v12

--- a/solution.py
+++ b/solution.py
@@ -8,6 +8,7 @@
 AUX = ("aux_x", "aux_y", "aux_core")
 NP = 4
 NZ = 16
+RINGS = [list(range(NZ)), list(range(2 * NZ - 1, NZ - 1, -1))]
 SCALE = 2.0**14
 V = 128
 AB = 128
@@ -23,8 +24,7 @@
         copy.start()
     va = virt[...]
     vb[...] = jnp.broadcast_to(va, (V, V)).T
-    for copy in copies:
-        copy.wait()
+    copies[0].wait()
     h = lax.axis_index("blk_y")
     w = lax.axis_index("blk_z")
     rows = lax.broadcasted_iota(jnp.int32, (NA, V), 0)
@@ -40,7 +40,10 @@
         pcat_t[s * V : (s + 1) * V, :] = block.T
     place = lax.broadcasted_iota(jnp.int32, here.shape, 1)
     here[...] = (place == lax.axis_index("aux_core")).astype(jnp.int32)
-    q_index = [h * NZ + k for k in range(NZ)]
+    copies[1].wait()
+    copies[2].wait()
+    core = lax.axis_index("aux_core")
+    q_index = [h * NZ + jnp.where(core == 0, k, NZ - 1 - k) for k in range(NZ)]
     qs, ts = [], []
     for c in range(0, NZ, 2):
         block = jnp.concatenate([jnp.where(live(q_index[c + t]), q_ref[c + t], zero) for t in range(2)], axis=1)
@@ -102,7 +105,7 @@
         -virt_energy,
     )
     sent, *scalars = lax.optimization_barrier((sent, *scalars))
-    line = lax.all_gather(sent, "blk_z", axis=0, tiled=True)
+    line = lax.all_gather(sent, ("aux_core", "blk_z"), axis=0, tiled=True, axis_index_groups=RINGS)
     part, here = pair_terms(scalars, p_blocks, line.astype(jnp.bfloat16))
     back = lax.all_to_all(part.reshape(32, 32, V), ("blk_y",) + AUX[:2], 0, 0, tiled=True)
     total = back.reshape(NP, 8, 2, 16, V).sum(axis=0)

time: 97.3 us -> 97.2 us (level)
  no operation moved by 1% of the time
where the time goes in v14:
time: 97.2 us; the launch traced here: 96.8 us
  blocking collectives  52.5 us (54%)
  starting transfers between devices  32.8 us (34%)
  waiting for transfers between devices  4.76 us (5%)
  Pallas kernels  2.99 us (3%)
  local copies, waits for them, and re-layouts  2.7 us (3%)
    all_gather x1, blocking collectives, on_device(): lax.all_gather(sent, ('aux_core', 'blk_z'), axis=0, tiled=True, axis_inde...  32.6 us
    all_to_all x1, blocking collectives, on_device(): lax.all_to_all(part.reshape(32, 32, V), ('blk_y',) + AUX[:2], 0, 0, tiled...  19.9 us
    all_to_all x1, starting transfers between devices, on_device(): own = lax.all_to_all(b_tensor[0], AUX, 0, 0, tiled=True).reshape(1, NA, V)  17.6 us
    ppermute x1, starting transfers between devices, on_device(): lax.ppermute(jnp.where(here[:, 0] > 0, total[:, 1], total[:, 0]), 'aux_co...  11.8 us
    all_to_all x1, waiting for transfers between devices, on_device(): own = lax.all_to_all(b_tensor[0], AUX, 0, 0, tiled=True).reshape(1, NA, V)  3.88 us
    all_to_all x1, starting transfers between devices, on_device(): lax.all_to_all(jnp.broadcast_to(own, (NP, NA, V)), 'blk_y', 0, 0, tiled=T...  3.4 us
    pallas_call x1, Pallas kernels, pair_terms(): pl.pallas_call(pair_kernel, out_shape=(jax.ShapeDtypeStruct((NP, 16, 16,...  2.99 us
    unnamed x8, local copies, waits for them, and re-layouts  1.97 us
  transfers between devices with their start and end apart: 3, of which 2 were waited for; matrix products, arithmetic and copies ran while one was open for 0% of the time, Pallas kernels for 0%

profile of v14, /device:TPU:1, one launch (start us, length us, event | category | flops | bytes accessed | tf_op | source)
XLA Modules:
  0.0 96.8 jit_solution(10349042355588283078)
XLA Ops:
  0.0 0.0 copy-start
  0.0 17.6 %all-to-all-start = ((bf16[16,16,128]{2,1,0:T(8,128)(2,1)}), bf16[16,16,128]{2,1,0:T(8,128)(2,1)S(1)}, u32[]{:S(2)}, u32[]{:S(2)}) async-start(bf16[16,16,128]{2,1,0:T(8,128)(2,1)} %bitcast.20), calls=%async_computation | async-start | bytes 131072 | tf_op jit(solution)/shard_map/all_to_all | solution.py:98
  17.6 0.0 copy-done
  17.6 0.0 copy-start.1
  17.6 0.7 copy-done.1
  18.3 0.0 copy-start.2
  18.3 0.7 copy-done.2
  18.9 0.0 copy-start.3
  18.9 0.7 copy-done.3
  19.6 3.9 %all-to-all-done = bf16[16,16,128]{2,1,0:T(8,128)(2,1)S(1)} async-done(((bf16[16,16,128]{2,1,0:T(8,128)(2,1)}), bf16[16,16,128]{2,1,0:T(8,128)(2,1)S(1)}, u32[]{:S(2)}, u32[]{:S(2)}) %all-to-all-start) | async-done | bytes 65568 | tf_op jit(solution)/shard_map/all_to_all | solution.py:98
  23.5 0.7 broadcast_in_dim.17
  24.2 3.4 %all-to-all-start.1 = ((bf16[4,256,128]{2,1,0:T(8,128)(2,1)}), bf16[4,256,128]{2,1,0:T(8,128)(2,1)S(1)}, u32[]{:S(2)}, u32[]{:S(2)}) async-start(bf16[4,256,128]{2,1,0:T(8,128)(2,1)} %broadcast_in_dim.17), calls=%async_computation.1 | async-start | bytes 524288 | tf_op jit(solution)/shard_map/all_to_all | solution.py:99
  27.6 32.6 %all-gather.1 = f16[16,256,128]{2,1,0:T(8,128)(2,1)S(1)} all-gather(f16[1,256,128]{2,1,0:T(8,128)(2,1)S(1)} %bitcast.19), channel_id=1, replica_groups={{0,1,2,3,4,5,6,7,8,9,10,11,12,13,14,15},{79,78,77,76,75,74,73,72,71,70,..., dimensions={0}, use_global_device_ids=true | all-gather | bytes 1114112 | tf_op jit(solution)/shard_map/all_gather | solution.py:108
  60.2 0.2 convert_element_type.52.q_ref
  60.4 0.0 all-to-all-done.1.p_ref
  60.4 3.0 %shard_map.55 = (f32[4,16,16,128]{3,2,1,0:T(8,128)S(1)}, s32[8,2,16,128]{3,2,1,0:T(8,128)S(1)}) custom-call(f32[2,64]{1,0:T(2,128)S(1)} %convert_bitcast_fusion.1.sig_hbm, f32[64,64]{1,0:T(8,128)S(1)} %convert_bitcast_fusion.keep_hbm, f32[1,64]{1,0:T(1,128)S(1)} %negate_bitcast_fusion.occ_hbm, f32[1,128]{1,0:T(1,128)S(1)} %neg.19.virt, ...), custom_call_target="tpu_custom_call" | custom-call | flops 2000000000 | bytes 2000000 | tf_op jit(solution)/shard_map/pallas_call | solution.py:75
  63.4 19.9 %all_to_all.15 = f32[32,32,128]{2,1,0:T(8,128)S(1)} all-to-all(f32[32,32,128]{2,1,0:T(8,128)S(1)} %bitcast.16), channel_id=1, replica_groups=mesh['aux_x'=4,'aux_y'=2,'aux_core'=2,'blk_y'=4,'blk_z'=16] {'blk_y','au..., dimensions={0} | all-to-all | bytes 1048576 | tf_op jit(solution)/shard_map/all_to_all | solution.py:110
  83.4 11.8 %collective-permute-start = (f32[8,16,128]{2,1,0:T(8,128)S(1)}, f32[8,16,128]{2,1,0:T(8,128)S(1)}, u32[]{:S(2)}, u32[]{:S(2)}) collective-permute-start(f32[8,16,128]{2,1,0:T(8,128)S(1)} %fusion), channel_id=1, source_target_pairs={{0,64},{64,0},{1,65},{65,1},{2,66},{66,2},{3,67},{67,3},{4,68},{68... | collective-permute-start | bytes 196616 | tf_op jit(solution)/shard_map/ppermute | solution.py:112
  95.2 0.9 collective-permute-done
  96.1 0.7 compare_select_fusion
  (7 shorter events, 0.1 us)
Async XLA Ops:
  0.0 17.6 %copy-start = (s32[1,64,64]{2,1,0:T(8,128)S(1)}, s32[1,64,64]{2,1,0:T(8,128)}, u32[]{:S(2)}) copy-start(s32[1,64,64]{2,1,0:T(8,128)} %param.7) | copy-start | bytes 49156
  0.0 23.5 %all-to-all-start = ((bf16[16,16,128]{2,1,0:T(8,128)(2,1)}), bf16[16,16,128]{2,1,0:T(8,128)(2,1)S(1)}, u32[]{:S(2)}, u32[]{:S(2)}) async-start(bf16[16,16,128]{2,1,0:T(8,128)(2,1)} %bitcast.20), calls=%async_computation | async-start | bytes 131072 | tf_op jit(solution)/shard_map/all_to_all | solution.py:98
  17.6 0.7 copy-start.1
  18.3 0.7 copy-start.2
  18.9 0.7 copy-start.3
  24.2 36.2 %all-to-all-start.1 = ((bf16[4,256,128]{2,1,0:T(8,128)(2,1)}), bf16[4,256,128]{2,1,0:T(8,128)(2,1)S(1)}, u32[]{:S(2)}, u32[]{:S(2)}) async-start(bf16[4,256,128]{2,1,0:T(8,128)(2,1)} %broadcast_in_dim.17), calls=%async_computation.1 | async-start | bytes 524288 | tf_op jit(solution)/shard_map/all_to_all | solution.py:99
  83.4 12.7 %collective-permute-start = (f32[8,16,128]{2,1,0:T(8,128)S(1)}, f32[8,16,128]{2,1,0:T(8,128)S(1)}, u32[]{:S(2)}, u32[]{:S(2)}) collective-permute-start(f32[8,16,128]{2,1,0:T(8,128)S(1)} %fusion), channel_id=1, source_target_pairs={{0,64},{64,0},{1,65},{65,1},{2,66},{66,2},{3,67},{67,3},{4,68},{68... | collective-permute-start | bytes 196616 | tf_op jit(solution)/shard_map/ppermute | solution.py:112
